TPU v7x, 512 devices: a whole 4x4x16 slice. The times are simulated.
512 devices in a mesh: dp: 32 (over z, core), tensor: 16 (over x, y).
Axes of the slice: x: 4, y: 4, z: 16, core: 2. Of those that a mesh axis runs over, the one named last changes fastest.
Arguments:
- buffer: float32 [8192, 26624], P('dp', 'tensor'), may hold values from -300 to 300
- factor: float32 [26624, 512], P('tensor', 'dp'), may hold values from -6 to 6
Outputs:
- momentum_new: float32 [8192, 26624], P('dp', 'tensor')
- update: bfloat16 [8192, 26624], P('dp', 'tensor')
- factor_new: float32 [26624, 512], P('tensor', 'dp')
All inputs are finite; a program needn't handle non-finite values.
Results may differ from a plain program's by a relative error of at most 0.0018.
Values sent between devices are 32-bit elements; how exact they have to be, the bound alone decides.
A program may use at most 64 MiB of HBM per device.

v0:
```python
import functools
import math

import jax
import jax.numpy as jnp
from jax import lax
from jax.experimental import pallas as pl
from jax.experimental.pallas import tpu as pltpu
from jax.sharding import PartitionSpec as P

MESH = pl.DeviceIdType.MESH
HIGHEST = lax.Precision.HIGHEST
NT = (((1,), (1,)), ((), ()))
NN = (((1,), (0,)), ((), ()))
LIMIT = 56 * 1024 * 1024


def dot(a, b, dims, precision):
    return lax.dot_general(
        a, b, dims, precision=precision, preferred_element_type=jnp.float32
    )


class Place:
    def __init__(self, chips, peers):
        dp = lax.axis_index("dp")
        self.z, self.c = dp // 2, dp % 2
        self.t = lax.axis_index("tensor")
        self.chips, self.peers = chips, peers

    def chip(self, offset):
        return lax.rem(self.z + offset + self.chips, self.chips)

    def at(self, offset):
        return {"dp": 2 * self.chip(offset) + self.c}

    def partner(self):
        return {"dp": 2 * self.z + 1 - self.c}

    def peer(self, k):
        return lax.rem(self.t + k, self.peers)


def remote(src, dst, send, recv, device):
    return pltpu.make_async_remote_copy(
        src_ref=src,
        dst_ref=dst,
        send_sem=send,
        recv_sem=recv,
        device_id=device,
        device_id_type=MESH,
    )


def await_bytes(ref, sem):
    pltpu.make_async_copy(ref, ref, sem).wait()


def enter(here, ring):
    barrier = pltpu.get_barrier_semaphore()

    def greet(device):
        pl.semaphore_signal(barrier, inc=1, device_id=device, device_id_type=MESH)

    @pl.loop(1, here.peers)
    def _(k):
        greet({"tensor": here.peer(k)})

    greet(here.partner())
    if ring:

        @pl.loop(1, here.chips)
        def _(k):
            greet(here.at(k))

        count = here.chips - 1
    else:
        greet(here.at(1))
        greet(here.at(-1))
        count = 2
    pl.semaphore_wait(barrier, here.peers - 1 + 1 + count)


def offset_of(n):
    return ((n + 1) // 2) * (2 * (n % 2) - 1)


def rows16(ref, chip, core, sub=None):
    start = 32 * chip + 16 * core
    if sub is None:
        return ref.at[pl.ds(pl.multiple_of(start, 16), 16)]
    return ref.at[pl.ds(pl.multiple_of(start + 8 * sub, 8), 8)]


class Gather:
    def __init__(self, here, buf, send, recv, pair_recv):
        self.here, self.buf = here, buf
        self.send, self.recv, self.pair_recv = send, recv, pair_recv
        self.half = here.chips // 2

    def subs(self, step, way):
        if step < self.half:
            return (0, 1)
        return (way,) if step == self.half else ()

    def forward(self, step, way, sub):
        here, sign = self.here, 1 - 2 * way
        ref = rows16(self.buf, here.chip(-sign * (step - 1)), here.c, sub)
        remote(
            ref, ref, self.send, self.recv.at[way, step - 1, sub], here.at(sign)
        ).start()

    def share(self, offset, slot):
        here = self.here
        ref = rows16(self.buf, here.chip(offset), here.c)
        remote(ref, ref, self.send, self.pair_recv.at[slot], here.partner()).start()

    def begin(self):
        for sub in (0, 1):
            for way in (0, 1):
                self.forward(1, way, sub)
        self.share(0, 0)

    def step(self, step):
        here = self.here
        for sub in (0, 1):
            for way in (0, 1):
                if sub in self.subs(step, way):
                    sign = 1 - 2 * way
                    ref = rows16(self.buf, here.chip(-sign * step), here.c, sub)
                    await_bytes(ref, self.recv.at[way, step - 1, sub])
                    if sub in self.subs(step + 1, way):
                        self.forward(step + 1, way, sub)
        if step < self.half:
            self.share(step, 2 * step - 1)
            self.share(-step, 2 * step)
        else:
            self.share(step, 2 * step - 1)

    def shared(self, n):
        here = self.here
        ref = rows16(self.buf, here.chip(offset_of(n)), 1 - here.c)
        await_bytes(ref, self.pair_recv.at[n])

    def end(self):
        rows = 16 * (2 * self.here.chips - 1)
        await_bytes(self.buf.at[pl.ds(0, rows)], self.send)


def split(value):
    high = value.astype(jnp.bfloat16)
    return high, (value - high.astype(jnp.float32)).astype(jnp.bfloat16)


def dot3(a, b, dims):
    return (
        dot(a[0], b[0], dims, None) + dot(a[0], b[1], dims, None)
    ) + dot(a[1], b[0], dims, None)


def splat(value):
    return jnp.broadcast_to(value, (8, 128))


def eliminate(m, carry, w_ref, start):
    s, x = carry
    columns = [jnp.broadcast_to(s[:, j : j + 1], s.shape) for j in range(8)]
    d = {(i, j): splat(columns[j][i : i + 1, :]) for j in range(8) for i in range(j, 8)}
    r = [splat(s[i : i + 1, :]) for i in range(8)]
    q = [splat(x[i : i + 1, :]) for i in range(8)]
    inverse = []
    for k in range(8):
        inv = lax.rsqrt(d[k, k])
        inverse.append(inv)
        r[k] = r[k] * inv
        q[k] = q[k] * inv
        for i in range(k + 1, 8):
            d[i, k] = d[i, k] * inv
        for i in range(k + 1, 8):
            for j in range(k + 1, i + 1):
                d[i, j] = d[i, j] - d[i, k] * d[j, k]
            r[i] = r[i] - d[i, k] * r[k]
            q[i] = q[i] - d[i, k] * q[k]
    sublane = lax.broadcasted_iota(jnp.int32, (8, 128), 0)
    done = q[0]
    for k in range(1, 8):
        done = jnp.where(sublane == k, q[k], done)
    w_ref[pl.ds(pl.multiple_of(start + 8 * m, 8), 8), start : start + 128] = done
    for k in range(7, -1, -1):
        for i in range(k + 1, 8):
            r[k] = r[k] - d[i, k] * r[i]
            q[k] = q[k] - d[i, k] * q[i]
        r[k] = r[k] * inverse[k]
        q[k] = q[k] * inverse[k]
    s, x = s[8:], x[8:]
    for j in range(8):
        c = columns[j][8:]
        s = s - c * r[j][0:1, :]
        x = x - c * q[j][0:1, :]
    blank = jnp.zeros((8, 128), jnp.float32)
    s = pltpu.roll(jnp.concatenate([s, blank], axis=0), 120, 1)
    return s, jnp.concatenate([x, blank], axis=0)


def invert_factor(a_ref, w_ref, between, after):
    rank = a_ref.shape[0]
    rows = lax.broadcasted_iota(jnp.int32, (128, 128), 0)
    lanes = lax.broadcasted_iota(jnp.int32, (128, 128), 1)
    w_ref[...] = jnp.zeros_like(w_ref)
    for start in range(0, rank, 128):
        stop = start + 128
        here = slice(start, stop)
        carry = (a_ref[here, here], jnp.where(rows == lanes, 1.0, 0.0).astype(jnp.float32))
        for quarter in range(4):
            carry = lax.fori_loop(
                4 * quarter,
                4 * quarter + 4,
                functools.partial(eliminate, w_ref=w_ref, start=start),
                carry,
            )
            between()
        w11 = w_ref[here, here]
        if start:
            w_ref[here, 0:start] = dot(w11, w_ref[here, 0:start], NN, HIGHEST)
        if stop < rank:
            below = slice(stop, rank)
            lower = dot(a_ref[below, here], w11, NT, HIGHEST)
            a_ref[below, below] = a_ref[below, below] - dot(lower, lower, NT, HIGHEST)
            w_ref[below, 0:stop] = w_ref[below, 0:stop] - dot(
                lower, w_ref[here, 0:stop], NN, HIGHEST
            )
        after(here)


def column_tiles(columns):
    return [(at, min(256, columns - at)) for at in range(0, columns, 256)]


def kernel(
    chips,
    peers,
    scale,
    mean,
    gain,
    b_ref,
    f_ref,
    momentum_ref,
    update_ref,
    factor_ref,
    bsplit,
    fall,
    part,
    first_parts,
    last_parts,
    arrived,
    pt,
    psplit,
    gpart,
    gpair,
    gsplit,
    gsplits,
    gsums,
    gram,
    a_ref,
    w_ref,
    wsplit,
    rpart,
    rpair,
    moving,
    rall,
    rsplit,
    squares,
    f_send,
    f_recv,
    f_pair,
    p_send,
    p_recv,
    g_send,
    g_recv,
    pair_send,
    pair_recv,
    rs_send,
    rs_recv,
    ag_send,
    ag_recv,
    ag_pair,
    sq_send,
    sq_recv,
):
    here = Place(chips, peers)
    rank = 32 * chips
    ring = chips // 2
    groups = chips // 4
    last = groups - 1
    tiles = column_tiles(b_ref.shape[1])
    own = rows16(fall, here.z, here.c)
    own[...] = f_ref[...]
    enter(here, True)
    gather = Gather(here, fall, f_send, f_recv, f_pair)
    gather.begin()
    bsplit[0], bsplit[1] = split(b_ref[...])

    def product(g):
        for n in range(4 * g, 4 * g + 4):
            gather.shared(n)
        rows = [
            fall[pl.ds(pl.multiple_of(32 * here.chip(offset_of(n)), 32), 32), :]
            for n in range(4 * g, 4 * g + 4)
        ]
        f = split(jnp.concatenate(rows, axis=0))
        part[128 * g : 128 * g + 128, :] = dot3(f, (bsplit[0], bsplit[1]), NT)

    def spread(base, rows, parts, turn):
        piece = rows // peers

        @pl.loop(1, peers)
        def _(k):
            other = here.peer(k)
            start = pl.multiple_of(base + piece * other, 8)
            remote(
                part.at[pl.ds(start, piece)],
                parts.at[k],
                p_send.at[turn],
                p_recv.at[turn],
                {"tensor": other},
            ).start()

    def total(base, rows, parts, turn):
        piece = rows // peers
        mine = pl.ds(pl.multiple_of(base + piece * here.t, 8), piece)
        parts[0] = part[mine, :]
        await_bytes(parts.at[pl.ds(1, peers - 1)], p_recv.at[turn])
        arrived[mine, :] = jnp.sum(parts[...], axis=0) * scale

        @pl.loop(1, peers)
        def _(k):
            place = arrived.at[mine]
            remote(
                place,
                place,
                p_send.at[turn + 1],
                p_recv.at[turn + 1],
                {"tensor": here.peer(k)},
            ).start()

    early = 128 * last
    for step in range(1, ring + 1):
        gather.step(step)
        if step % 2 == 0:
            product(step // 2 - 1)
            if step // 2 == last:
                spread(0, early, first_parts, 0)
        elif last and step == ring - 1:
            total(0, early, first_parts, 0)
    spread(early, 128, last_parts, 2)
    total(early, 128, last_parts, 2)
    if last:
        await_bytes(first_parts.at[pl.ds(1, peers - 1)], p_recv.at[1])
    await_bytes(last_parts.at[pl.ds(1, peers - 1)], p_recv.at[3])
    for n in range(chips):
        place = pl.ds(pl.multiple_of(32 * here.chip(offset_of(n)), 32), 32)
        pt[place, :] = arrived[32 * n : 32 * n + 32, :]

    def right_product(g):
        chipped = [here.chip(offset_of(n)) for n in range(4 * g, 4 * g + 4)]
        p = split(arrived[128 * g : 128 * g + 128, :])
        for at, width in tiles:
            b = (bsplit[0, :, at : at + width], bsplit[1, :, at : at + width])
            r = dot3(p, b, NN)
            for n, i in enumerate(chipped):
                place = pl.ds(pl.multiple_of(32 * i, 32), 32)
                rpart[place, at : at + width] = r[32 * n : 32 * n + 32, :]
        for n, i in enumerate(chipped):
            remote(
                rows16(rpart, i, 1 - here.c),
                rpair.at[4 * g + n],
                pair_send,
                pair_recv.at[g],
                here.partner(),
            ).start()

    def right_own(n, sub):
        chip = here.chip(offset_of(n))
        return rows16(rpart, chip, here.c, sub)[...] + rpair[n, 8 * sub : 8 * sub + 8, :]

    def scatter(k):
        if k % 2 == 0:
            g = k // 2 - 1
            await_bytes(rpair.at[pl.ds(4 * g, 4)], pair_recv.at[g])
        for sub in (0, 1):
            for way in (0, 1):
                if k == ring and sub != way:
                    continue
                place = moving.at[way, k, pl.ds(8 * sub, 8)]
                n = 2 * k - 1 if (way == 0 or k == ring) else 2 * k
                if k < ring - 1 or (k == ring - 1 and sub == way):
                    await_bytes(place, rs_recv.at[way, k, sub])
                    place[...] = place[...] + right_own(n, sub)
                else:
                    place[...] = right_own(n, sub)
                remote(
                    place,
                    moving.at[way, k - 1, pl.ds(8 * sub, 8)],
                    rs_send,
                    rs_recv.at[way, k - 1, sub],
                    here.at(1 - 2 * way),
                ).start()

    collect = Gather(here, rall, ag_send, ag_recv, ag_pair)

    def settle():
        for sub in (0, 1):
            for way in (0, 1):
                place = moving.at[way, 0, pl.ds(8 * sub, 8)]
                await_bytes(place, rs_recv.at[way, 0, sub])
            rows16(rall, here.z, here.c, sub)[...] = (
                right_own(0, sub)
                + moving[0, 0, 8 * sub : 8 * sub + 8, :]
                + moving[1, 0, 8 * sub : 8 * sub + 8, :]
            )
        collect.begin()

    def halve(n):
        collect.shared(n)
        place = pl.ds(pl.multiple_of(32 * here.chip(offset_of(n)), 32), 32)
        rsplit[0, place, :], rsplit[1, place, :] = split(rall[place, :])

    def onward(step):
        collect.step(step)
        if step == 1:
            halve(0)
        else:
            halve(2 * step - 3)
            halve(2 * step - 2)

    events = []
    for g in range(last, -1, -1):
        events.append(functools.partial(right_product, g))
        events.append(functools.partial(scatter, 2 * g + 2))
        events.append(functools.partial(scatter, 2 * g + 1))
    events.append(settle)
    events += [functools.partial(onward, step) for step in range(1, ring + 1)]
    events.reverse()

    def advance(count=1):
        for _ in range(count):
            if events:
                events.pop()()

    advance()
    block = rank // peers
    half = block // 2
    each = half // chips
    mine = pl.ds(pl.multiple_of(block * here.t, block), block)
    gpart[...] = dot(pt[mine, :], pt[...], NT, HIGHEST)
    theirs = pl.ds(pl.multiple_of(half * (1 - here.c), half), half)
    keep = pl.ds(pl.multiple_of(half * here.c, half), half)
    pair = remote(gpart.at[theirs], gpair, g_send.at[0], g_recv.at[0], here.partner())
    pair.start()
    advance()
    psplit[0], psplit[1] = split(pt[...].T)
    pair.wait()
    chip_sum = gpart[keep, :] + gpair[...]
    for k in range(chips):
        gsplit[k] = chip_sum[each * k : each * (k + 1), :]

    @pl.loop(1, chips)
    def _(k):
        remote(
            gsplit.at[here.chip(k)],
            gsplits.at[k],
            g_send.at[1],
            g_recv.at[1],
            here.at(k),
        ).start()

    advance(2)
    gsplits[0] = gsplit[here.z]
    await_bytes(gsplits.at[pl.ds(1, chips - 1)], g_recv.at[1])
    gsums[here.z] = jnp.sum(gsplits[...], axis=0)

    @pl.loop(1, chips)
    def _(k):
        place = gsums.at[here.z]
        remote(place, place, g_send.at[2], g_recv.at[2], here.at(k)).start()

    advance(2)
    await_bytes(gsums.at[pl.ds(0, chips - 1)], g_recv.at[2])
    gram[here.t, here.c] = gsums[...].reshape(half, rank)

    @pl.loop(1, peers)
    def _(k):
        place = gram.at[here.t, here.c]
        remote(
            place, place, g_send.at[3], g_recv.at[3], {"tensor": here.peer(k)}
        ).start()

    advance(2)
    await_bytes(gram.at[pl.ds(0, peers - 1), 0], g_recv.at[3])
    halves = gram.at[:, here.c]
    pair = remote(halves, halves, g_send.at[4], g_recv.at[4], here.partner())
    pair.start()
    advance()
    pair.wait()
    a_ref[...] = gram[...].reshape(rank, rank)

    def after(rows):
        wsplit[0, rows, :], wsplit[1, rows, :] = split(w_ref[rows, :])

    invert_factor(a_ref, w_ref, advance, after)
    advance(len(events))
    halve(chips - 1)

    await_bytes(rpart.at[pl.ds(0, rank // 2)], pair_send)
    sums = jnp.zeros((rank, 128), jnp.float32)
    for at, width in tiles:
        columns = slice(at, at + width)
        blocks = []
        for row in range(0, rank, 128):
            stop = row + 128
            blocks.append(
                dot3(
                    (wsplit[0, row:stop, 0:stop], wsplit[1, row:stop, 0:stop]),
                    (rsplit[0, 0:stop, columns], rsplit[1, 0:stop, columns]),
                    NN,
                )
            )
        right = jnp.concatenate(blocks, axis=0)
        rpart[:, columns] = right
        for lane in range(0, width, 128):
            one = right[:, lane : lane + 128]
            sums = sums + one * one
        rsplit[0, :, columns], rsplit[1, :, columns] = split(right)
    squares[0] = jnp.sum(sums.T, axis=0, keepdims=True)

    @pl.loop(1, peers)
    def _(k):
        remote(
            squares.at[0], squares.at[k], sq_send, sq_recv, {"tensor": here.peer(k)}
        ).start()

    q = dot3((psplit[0], psplit[1]), (wsplit[0], wsplit[1]), NT)
    q1 = (q * -0.05).astype(jnp.bfloat16)
    for at, width in tiles:
        columns = slice(at, at + width)
        momentum_ref[:, columns] = b_ref[:, columns] + dot(
            q1, rsplit[0, :, columns], NN, None
        )
    await_bytes(squares.at[pl.ds(1, peers - 1)], sq_recv)
    scales = lax.rsqrt(jnp.sum(squares[...], axis=0) * mean + 1e-06)
    scaled = split(q * (scales * gain))
    for at, width in tiles:
        columns = slice(at, at + width)
        update_ref[:, columns] = dot3(
            scaled, (rsplit[0, :, columns], rsplit[1, :, columns]), NN
        ).astype(jnp.bfloat16)
    lanes = lax.broadcasted_iota(jnp.int32, (16, rank), 1)
    rows = lax.broadcasted_iota(jnp.int32, (16, rank), 0) + (32 * here.z + 16 * here.c)
    picked = jnp.where(lanes == rows, jnp.broadcast_to(scales, (16, rank)), 0.0)
    factor_ref[...] = rows16(rpart, here.z, here.c)[...] * jnp.sum(
        picked, axis=1, keepdims=True
    )

    gather.end()
    collect.end()
    if last:
        for turn in (0, 1):
            await_bytes(first_parts.at[pl.ds(1, peers - 1)], p_send.at[turn])
    for turn in (2, 3):
        await_bytes(last_parts.at[pl.ds(1, peers - 1)], p_send.at[turn])
    await_bytes(gsplits.at[pl.ds(1, chips - 1)], g_send.at[1])
    await_bytes(gsums.at[pl.ds(0, chips - 1)], g_send.at[2])
    await_bytes(gram.at[pl.ds(0, peers - 1), 0], g_send.at[3])
    await_bytes(rall.at[pl.ds(0, 16 * (chips - 1))], rs_send)
    await_bytes(squares.at[pl.ds(1, peers - 1)], sq_send)


def body(chips, peers, buffer, factor):
    rows, columns = buffer.shape
    rank = 32 * chips
    half = rank // peers // 2
    each = half // chips
    total_columns = columns * peers
    groups = chips // 4
    ring = chips // 2
    f32, bf16 = jnp.float32, jnp.bfloat16
    dma = pltpu.SemaphoreType.DMA
    vmem = pl.BlockSpec(memory_space=pltpu.VMEM)
    momentum, update, factor_t = pl.pallas_call(
        functools.partial(
            kernel,
            chips,
            peers,
            1.0 / math.sqrt(total_columns),
            1.0 / total_columns,
            math.sqrt(rows * 2 * chips / rank),
        ),
        out_shape=(
            jax.ShapeDtypeStruct((rows, columns), f32),
            jax.ShapeDtypeStruct((rows, columns), bf16),
            jax.ShapeDtypeStruct((16, columns), f32),
        ),
        in_specs=[vmem] * 2,
        out_specs=(vmem,) * 3,
        scratch_shapes=[
            pltpu.VMEM((2, rows, columns), bf16),
            pltpu.VMEM((rank, columns), f32),
            pltpu.VMEM((rank, rows), f32),
            pltpu.VMEM((peers, max(groups - 1, 1) * 128 // peers, rows), f32),
            pltpu.VMEM((peers, 128 // peers, rows), f32),
            pltpu.VMEM((rank, rows), f32),
            pltpu.VMEM((rank, rows), f32),
            pltpu.VMEM((2, rows, rank), bf16),
            pltpu.VMEM((2 * half, rank), f32),
            pltpu.VMEM((half, rank), f32),
            pltpu.VMEM((chips, each, rank), f32),
            pltpu.VMEM((chips, each, rank), f32),
            pltpu.VMEM((chips, each, rank), f32),
            pltpu.VMEM((peers, 2, half, rank), f32),
            pltpu.VMEM((rank, rank), f32),
            pltpu.VMEM((rank, rank), f32),
            pltpu.VMEM((2, rank, rank), bf16),
            pltpu.VMEM((rank, columns), f32),
            pltpu.VMEM((chips, 16, columns), f32),
            pltpu.VMEM((2, ring + 1, 16, columns), f32),
            pltpu.VMEM((rank, columns), f32),
            pltpu.VMEM((2, rank, columns), bf16),
            pltpu.VMEM((peers, 1, rank), f32),
            dma,
            dma((2, ring, 2)),
            dma((chips,)),
            dma((4,)),
            dma((4,)),
            dma((5,)),
            dma((5,)),
            dma,
            dma((groups,)),
            dma,
            dma((2, ring, 2)),
            dma,
            dma((2, ring, 2)),
            dma((chips,)),
            dma,
            dma,
        ],
        compiler_params=pltpu.CompilerParams(
            collective_id=0, has_side_effects=True, vmem_limit_bytes=LIMIT
        ),
        name="low_rank_update",
    )(buffer, factor.T)
    return momentum, update, factor_t.T


def solution(mesh):
    chips, peers = mesh.shape["dp"] // 2, mesh.shape["tensor"]
    placed = (P("dp", "tensor"), P("tensor", "dp"))
    return jax.shard_map(
        functools.partial(body, chips, peers),
        mesh=mesh,
        in_specs=placed,
        out_specs=(P("dp", "tensor"), P("dp", "tensor"), P("tensor", "dp")),
        check_vma=False,
    )
```

profile of v0, /device:TPU:1, one launch (start us, length us, event | category | flops | bytes accessed | tf_op | source)
XLA Modules:
  0.0 158.5 jit_solution(5443372692065484365)
XLA Ops:
  0.6 153.5 %low_rank_update.1 = (f32[256,1664]{1,0:T(8,128)}, bf16[256,1664]{1,0:T(8,128)(2,1)}, f32[16,1664]{1,0:T(8,128)}) custom-call(f32[256,1664]{1,0:T(8,128)} %b_ref.1, f32[16,1664]{1,0:T(8,128)} %bitcast.2), custom_call_target="tpu_custom_call" | custom-call | tf_op jit(solution)/shard_map/low_rank_update/pallas_call | solution.py:589
  154.1 0.0 copy-start
  154.2 0.0 copy-start.1
  154.2 2.8 %copy.8 = f32[256,1664]{1,0:T(8,128)} copy(f32[256,1664]{1,0:T(8,128)} %get-tuple-element.12) | data formatting | bytes 3407872
  157.0 0.0 copy-done
  157.0 0.9 copy.9
  157.9 0.0 copy-done.1
  157.9 0.6 copy.10
Async XLA Ops:
  154.1 2.9 %copy-start = (bf16[256,1664]{1,0:T(8,128)(2,1)S(1)}, bf16[256,1664]{1,0:T(8,128)(2,1)}, u32[]{:S(2)}) copy-start(bf16[256,1664]{1,0:T(8,128)(2,1)} %get-tuple-element.13) | copy-start | bytes 2555908
  154.2 3.7 %copy-start.1 = (f32[16,1664]{1,0:T(8,128)S(1)}, f32[16,1664]{1,0:T(8,128)}, u32[]{:S(2)}) copy-start(f32[16,1664]{1,0:T(8,128)} %get-tuple-element.8) | copy-start | bytes 319492
where the time goes:
time: 160 us; the launch traced here: 159 us
  Pallas kernels  154 us (96%)
  local copies, waits for them, and re-layouts  4.38 us (3%)
    pallas_call x1, Pallas kernels, body(): pl.pallas_call(functools.partial(kernel, chips, peers, 1.0 / math.sqrt(to...  154 us
    unnamed x7, local copies, waits for them, and re-layouts  4.38 us

commit v1 on v0

--- a/solution.py
+++ b/solution.py
@@ -10,7 +10,6 @@
 
 MESH = pl.DeviceIdType.MESH
 HIGHEST = lax.Precision.HIGHEST
-NT = (((1,), (1,)), ((), ()))
 NN = (((1,), (0,)), ((), ()))
 LIMIT = 56 * 1024 * 1024
 
@@ -162,74 +161,76 @@
     return jnp.broadcast_to(value, (8, 128))
 
 
-def eliminate(m, carry, w_ref, start):
-    s, x = carry
-    columns = [jnp.broadcast_to(s[:, j : j + 1], s.shape) for j in range(8)]
-    d = {(i, j): splat(columns[j][i : i + 1, :]) for j in range(8) for i in range(j, 8)}
-    r = [splat(s[i : i + 1, :]) for i in range(8)]
-    q = [splat(x[i : i + 1, :]) for i in range(8)]
-    inverse = []
-    for k in range(8):
-        inv = lax.rsqrt(d[k, k])
-        inverse.append(inv)
-        r[k] = r[k] * inv
-        q[k] = q[k] * inv
-        for i in range(k + 1, 8):
-            d[i, k] = d[i, k] * inv
-        for i in range(k + 1, 8):
-            for j in range(k + 1, i + 1):
-                d[i, j] = d[i, j] - d[i, k] * d[j, k]
-            r[i] = r[i] - d[i, k] * r[k]
-            q[i] = q[i] - d[i, k] * q[k]
+def eliminate(turn, carry, w_ref):
+    s = carry
+    lane = lax.broadcasted_iota(jnp.int32, (8, 128), 1)
     sublane = lax.broadcasted_iota(jnp.int32, (8, 128), 0)
-    done = q[0]
-    for k in range(1, 8):
-        done = jnp.where(sublane == k, q[k], done)
-    w_ref[pl.ds(pl.multiple_of(start + 8 * m, 8), 8), start : start + 128] = done
-    for k in range(7, -1, -1):
-        for i in range(k + 1, 8):
-            r[k] = r[k] - d[i, k] * r[i]
-            q[k] = q[k] - d[i, k] * q[i]
-        r[k] = r[k] * inverse[k]
-        q[k] = q[k] * inverse[k]
-    s, x = s[8:], x[8:]
-    for j in range(8):
-        c = columns[j][8:]
-        s = s - c * r[j][0:1, :]
-        x = x - c * q[j][0:1, :]
-    blank = jnp.zeros((8, 128), jnp.float32)
-    s = pltpu.roll(jnp.concatenate([s, blank], axis=0), 120, 1)
-    return s, jnp.concatenate([x, blank], axis=0)
-
-
-def invert_factor(a_ref, w_ref, between, after):
-    rank = a_ref.shape[0]
-    rows = lax.broadcasted_iota(jnp.int32, (128, 128), 0)
-    lanes = lax.broadcasted_iota(jnp.int32, (128, 128), 1)
-    w_ref[...] = jnp.zeros_like(w_ref)
+    for half in (0, 8):
+        block = (lane >= half) & (lane < half + 8)
+        columns = [
+            jnp.broadcast_to(s[:, half + j : half + j + 1], s.shape) for j in range(8)
+        ]
+        d = {
+            (i, j): splat(columns[j][i : i + 1, :]) for j in range(8) for i in range(j, 8)
+        }
+        top = jnp.where(block, jnp.where(lane == sublane + half, 1.0, 0.0), s[0:8])
+        r = [splat(top[i : i + 1, :]) for i in range(8)]
+        root, inverse, t = [], [], {}
+        for k in range(8):
+            root.append(lax.rsqrt(d[k, k]))
+            inverse.append(root[k] * root[k])
+            for i in range(k + 1, 8):
+                t[i, k] = d[i, k] * inverse[k]
+                for j in range(k + 1, i + 1):
+                    d[i, j] = d[i, j] - t[i, k] * d[j, k]
+                r[i] = r[i] - t[i, k] * r[k]
+        done = r[0] * root[0]
+        for k in range(1, 8):
+            done = jnp.where(sublane == k, r[k] * root[k], done)
+        keep = (lane >= 128 - 16 * turn) | (lane < half + 8)
+        w_ref[pl.ds(pl.multiple_of(16 * turn + half, 8), 8), :] = jnp.where(
+            keep, done, 0.0
+        )
+        for k in range(7, -1, -1):
+            r[k] = r[k] * inverse[k]
+            for i in range(7, k, -1):
+                r[k] = r[k] - t[i, k] * r[i]
+        lanes = lax.broadcasted_iota(jnp.int32, (s.shape[0] - 8, 128), 1)
+        s = jnp.where((lanes >= half) & (lanes < half + 8), 0.0, s[8:])
+        for j in range(8):
+            s = s - columns[j][8:] * r[j][0:1, :]
+    blank = jnp.zeros((16, 128), jnp.float32)
+    return pltpu.roll(jnp.concatenate([s, blank], axis=0), 112, 1)
+
+
+def invert_factor(m_ref, block_ref, between, after):
+    rank = m_ref.shape[0]
     for start in range(0, rank, 128):
         stop = start + 128
         here = slice(start, stop)
-        carry = (a_ref[here, here], jnp.where(rows == lanes, 1.0, 0.0).astype(jnp.float32))
+        carry = m_ref[here, here]
         for quarter in range(4):
             carry = lax.fori_loop(
-                4 * quarter,
-                4 * quarter + 4,
-                functools.partial(eliminate, w_ref=w_ref, start=start),
+                2 * quarter,
+                2 * quarter + 2,
+                functools.partial(eliminate, w_ref=block_ref),
                 carry,
             )
             between()
-        w11 = w_ref[here, here]
-        if start:
-            w_ref[here, 0:start] = dot(w11, w_ref[here, 0:start], NN, HIGHEST)
+        w = [
+            pltpu.roll(block_ref[16 * i : 16 * i + 16, :], 16 * i, 1) if i else block_ref[0:16, :]
+            for i in range(8)
+        ]
+        w = jnp.concatenate(w, axis=0)
+        if rank > 128:
+            m_ref[here, :] = dot(w, m_ref[here, :], NN, HIGHEST)
+        m_ref[here, here] = w
         if stop < rank:
             below = slice(stop, rank)
-            lower = dot(a_ref[below, here], w11, NT, HIGHEST)
-            a_ref[below, below] = a_ref[below, below] - dot(lower, lower, NT, HIGHEST)
-            w_ref[below, 0:stop] = w_ref[below, 0:stop] - dot(
-                lower, w_ref[here, 0:stop], NN, HIGHEST
-            )
-        after(here)
+            lower = m_ref[here, below].T
+            m_ref[below, here] = jnp.zeros((rank - stop, 128), jnp.float32)
+            m_ref[below, :] = m_ref[below, :] - dot(lower, m_ref[here, :], NN, HIGHEST)
+        after(start, m_ref[here, 0:stop])
 
 
 def column_tiles(columns):
@@ -248,6 +249,7 @@
     update_ref,
     factor_ref,
     bsplit,
+    tsplit,
     fall,
     part,
     first_parts,
@@ -261,8 +263,8 @@
     gsplits,
     gsums,
     gram,
-    a_ref,
-    w_ref,
+    m_ref,
+    block_ref,
     wsplit,
     rpart,
     rpair,
@@ -298,6 +300,7 @@
     enter(here, True)
     gather = Gather(here, fall, f_send, f_recv, f_pair)
     gather.begin()
+    tsplit[0], tsplit[1] = split(b_ref[...].T)
     bsplit[0], bsplit[1] = split(b_ref[...])
 
     def product(g):
@@ -308,7 +311,7 @@
             for n in range(4 * g, 4 * g + 4)
         ]
         f = split(jnp.concatenate(rows, axis=0))
-        part[128 * g : 128 * g + 128, :] = dot3(f, (bsplit[0], bsplit[1]), NT)
+        part[128 * g : 128 * g + 128, :] = dot3(f, (tsplit[0], tsplit[1]), NN)
 
     def spread(base, rows, parts, turn):
         piece = rows // peers
@@ -452,13 +455,13 @@
     half = block // 2
     each = half // chips
     mine = pl.ds(pl.multiple_of(block * here.t, block), block)
-    gpart[...] = dot(pt[mine, :], pt[...], NT, HIGHEST)
+    gpart[...] = dot(pt[mine, :], pt[...].T, NN, HIGHEST)
     theirs = pl.ds(pl.multiple_of(half * (1 - here.c), half), half)
     keep = pl.ds(pl.multiple_of(half * here.c, half), half)
     pair = remote(gpart.at[theirs], gpair, g_send.at[0], g_recv.at[0], here.partner())
     pair.start()
     advance()
-    psplit[0], psplit[1] = split(pt[...].T)
+    psplit[0], psplit[1] = split(pt[...])
     pair.wait()
     chip_sum = gpart[keep, :] + gpair[...]
     for k in range(chips):
@@ -502,12 +505,14 @@
     pair.start()
     advance()
     pair.wait()
-    a_ref[...] = gram[...].reshape(rank, rank)
-
-    def after(rows):
-        wsplit[0, rows, :], wsplit[1, rows, :] = split(w_ref[rows, :])
-
-    invert_factor(a_ref, w_ref, advance, after)
+    m_ref[...] = gram[...].reshape(rank, rank)
+    wsplit[...] = jnp.zeros_like(wsplit)
+
+    def after(start, w):
+        rows, columns = slice(start, start + 128), slice(0, start + 128)
+        wsplit[0, rows, columns], wsplit[1, rows, columns] = split(w)
+
+    invert_factor(m_ref, block_ref, advance, after)
     advance(len(events))
     halve(chips - 1)
 
@@ -516,8 +521,8 @@
     for at, width in tiles:
         columns = slice(at, at + width)
         blocks = []
-        for row in range(0, rank, 128):
-            stop = row + 128
+        for row in range(0, rank, 256):
+            stop = row + 256
             blocks.append(
                 dot3(
                     (wsplit[0, row:stop, 0:stop], wsplit[1, row:stop, 0:stop]),
@@ -539,7 +544,17 @@
             squares.at[0], squares.at[k], sq_send, sq_recv, {"tensor": here.peer(k)}
         ).start()
 
-    q = dot3((psplit[0], psplit[1]), (wsplit[0], wsplit[1]), NT)
+    blocks = []
+    for row in range(0, rank, 256):
+        stop = row + 256
+        blocks.append(
+            dot3(
+                (wsplit[0, row:stop, 0:stop], wsplit[1, row:stop, 0:stop]),
+                (psplit[0, 0:stop, :], psplit[1, 0:stop, :]),
+                NN,
+            )
+        )
+    q = jnp.concatenate(blocks, axis=0).T
     q1 = (q * -0.05).astype(jnp.bfloat16)
     for at, width in tiles:
         columns = slice(at, at + width)
@@ -604,13 +619,14 @@
         out_specs=(vmem,) * 3,
         scratch_shapes=[
             pltpu.VMEM((2, rows, columns), bf16),
+            pltpu.VMEM((2, columns, rows), bf16),
             pltpu.VMEM((rank, columns), f32),
             pltpu.VMEM((rank, rows), f32),
             pltpu.VMEM((peers, max(groups - 1, 1) * 128 // peers, rows), f32),
             pltpu.VMEM((peers, 128 // peers, rows), f32),
             pltpu.VMEM((rank, rows), f32),
             pltpu.VMEM((rank, rows), f32),
-            pltpu.VMEM((2, rows, rank), bf16),
+            pltpu.VMEM((2, rank, rows), bf16),
             pltpu.VMEM((2 * half, rank), f32),
             pltpu.VMEM((half, rank), f32),
             pltpu.VMEM((chips, each, rank), f32),
@@ -618,7 +634,7 @@
             pltpu.VMEM((chips, each, rank), f32),
             pltpu.VMEM((peers, 2, half, rank), f32),
             pltpu.VMEM((rank, rank), f32),
-            pltpu.VMEM((rank, rank), f32),
+            pltpu.VMEM((128, 128), f32),
             pltpu.VMEM((2, rank, rank), bf16),
             pltpu.VMEM((rank, columns), f32),
             pltpu.VMEM((chips, 16, columns), f32),

time: 160 us -> 155 us (0.969)
  Pallas kernels: 154 us -> 148 us
    pallas_call x1, Pallas kernels: 154 us -> 148 us  [body(): pl.pallas_call(functools.partial(kernel, chips, peers, 1.0 / math.sqrt(to...]
where the time goes in v1:
time: 155 us; the launch traced here: 153 us
  Pallas kernels  148 us (95%)
  local copies, waits for them, and re-layouts  4.38 us (3%)
    pallas_call x1, Pallas kernels, body(): pl.pallas_call(functools.partial(kernel, chips, peers, 1.0 / math.sqrt(to...  148 us
    unnamed x7, local copies, waits for them, and re-layouts  4.38 us

profile of v1, /device:TPU:1, one launch (start us, length us, event | category | flops | bytes accessed | tf_op | source)
XLA Modules:
  0.0 153.3 jit_solution(4388990283340907752)
XLA Ops:
  0.6 148.3 %low_rank_update.1 = (f32[256,1664]{1,0:T(8,128)}, bf16[256,1664]{1,0:T(8,128)(2,1)}, f32[16,1664]{1,0:T(8,128)}) custom-call(f32[256,1664]{1,0:T(8,128)} %b_ref.1, f32[16,1664]{1,0:T(8,128)} %bitcast.2), custom_call_target="tpu_custom_call" | custom-call | tf_op jit(solution)/shard_map/low_rank_update/pallas_call | solution.py:604
  148.9 0.0 copy-start
  148.9 0.0 copy-start.1
  148.9 2.8 %copy.8 = f32[256,1664]{1,0:T(8,128)} copy(f32[256,1664]{1,0:T(8,128)} %get-tuple-element.12) | data formatting | bytes 3407872
  151.7 0.0 copy-done
  151.7 0.9 copy.9
  152.7 0.0 copy-done.1
  152.7 0.6 copy.10
Async XLA Ops:
  148.9 2.9 %copy-start = (bf16[256,1664]{1,0:T(8,128)(2,1)S(1)}, bf16[256,1664]{1,0:T(8,128)(2,1)}, u32[]{:S(2)}) copy-start(bf16[256,1664]{1,0:T(8,128)(2,1)} %get-tuple-element.13) | copy-start | bytes 2555908
  148.9 3.7 %copy-start.1 = (f32[16,1664]{1,0:T(8,128)S(1)}, f32[16,1664]{1,0:T(8,128)}, u32[]{:S(2)}) copy-start(f32[16,1664]{1,0:T(8,128)} %get-tuple-element.8) | copy-start | bytes 319492

commit v2 on v1

--- a/solution.py
+++ b/solution.py
@@ -120,21 +120,19 @@
                 self.forward(1, way, sub)
         self.share(0, 0)
 
-    def step(self, step):
+    def step(self, step, sub):
         here = self.here
-        for sub in (0, 1):
-            for way in (0, 1):
-                if sub in self.subs(step, way):
-                    sign = 1 - 2 * way
-                    ref = rows16(self.buf, here.chip(-sign * step), here.c, sub)
-                    await_bytes(ref, self.recv.at[way, step - 1, sub])
-                    if sub in self.subs(step + 1, way):
-                        self.forward(step + 1, way, sub)
-        if step < self.half:
+        for way in (0, 1):
+            if sub in self.subs(step, way):
+                sign = 1 - 2 * way
+                ref = rows16(self.buf, here.chip(-sign * step), here.c, sub)
+                await_bytes(ref, self.recv.at[way, step - 1, sub])
+                if sub in self.subs(step + 1, way):
+                    self.forward(step + 1, way, sub)
+        if sub == 1:
             self.share(step, 2 * step - 1)
-            self.share(-step, 2 * step)
-        else:
-            self.share(step, 2 * step - 1)
+            if step < self.half:
+                self.share(-step, 2 * step)
 
     def shared(self, n):
         here = self.here
@@ -161,75 +159,79 @@
     return jnp.broadcast_to(value, (8, 128))
 
 
-def eliminate(turn, carry, w_ref):
-    s = carry
+def eliminate(m, s, w_ref):
+    at, stop = 8 * m, 8 * m + 8
     lane = lax.broadcasted_iota(jnp.int32, (8, 128), 1)
     sublane = lax.broadcasted_iota(jnp.int32, (8, 128), 0)
-    for half in (0, 8):
-        block = (lane >= half) & (lane < half + 8)
-        columns = [
-            jnp.broadcast_to(s[:, half + j : half + j + 1], s.shape) for j in range(8)
-        ]
-        d = {
-            (i, j): splat(columns[j][i : i + 1, :]) for j in range(8) for i in range(j, 8)
-        }
-        top = jnp.where(block, jnp.where(lane == sublane + half, 1.0, 0.0), s[0:8])
-        r = [splat(top[i : i + 1, :]) for i in range(8)]
-        root, inverse, t = [], [], {}
-        for k in range(8):
-            root.append(lax.rsqrt(d[k, k]))
-            inverse.append(root[k] * root[k])
-            for i in range(k + 1, 8):
-                t[i, k] = d[i, k] * inverse[k]
-                for j in range(k + 1, i + 1):
-                    d[i, j] = d[i, j] - t[i, k] * d[j, k]
-                r[i] = r[i] - t[i, k] * r[k]
-        done = r[0] * root[0]
-        for k in range(1, 8):
-            done = jnp.where(sublane == k, r[k] * root[k], done)
-        keep = (lane >= 128 - 16 * turn) | (lane < half + 8)
-        w_ref[pl.ds(pl.multiple_of(16 * turn + half, 8), 8), :] = jnp.where(
-            keep, done, 0.0
-        )
-        for k in range(7, -1, -1):
-            r[k] = r[k] * inverse[k]
-            for i in range(7, k, -1):
-                r[k] = r[k] - t[i, k] * r[i]
-        lanes = lax.broadcasted_iota(jnp.int32, (s.shape[0] - 8, 128), 1)
-        s = jnp.where((lanes >= half) & (lanes < half + 8), 0.0, s[8:])
-        for j in range(8):
-            s = s - columns[j][8:] * r[j][0:1, :]
-    blank = jnp.zeros((16, 128), jnp.float32)
-    return pltpu.roll(jnp.concatenate([s, blank], axis=0), 112, 1)
+    columns = [jnp.broadcast_to(s[:, at + j : at + j + 1], s.shape) for j in range(8)]
+    d = {(i, j): splat(columns[j][i : i + 1, :]) for j in range(8) for i in range(j, 8)}
+    block = (lane >= at) & (lane < stop)
+    top = jnp.where(block, jnp.where(lane == sublane + at, 1.0, 0.0), s[0:8])
+    r = [splat(top[i : i + 1, :]) for i in range(8)]
+    root, inverse, t = [], [], {}
+    for k in range(8):
+        root.append(lax.rsqrt(d[k, k]))
+        inverse.append(root[k] * root[k])
+        for i in range(k + 1, 8):
+            t[i, k] = d[i, k] * inverse[k]
+            for j in range(k + 1, i + 1):
+                d[i, j] = d[i, j] - t[i, k] * d[j, k]
+            r[i] = r[i] - t[i, k] * r[k]
+    done = r[0] * root[0]
+    for k in range(1, 8):
+        done = jnp.where(sublane == k, r[k] * root[k], done)
+    w_ref[at:stop, :] = jnp.where(lane < stop, done, 0.0)
+    if m == 15:
+        return None
+    for k in range(7, -1, -1):
+        r[k] = r[k] * inverse[k]
+        for i in range(7, k, -1):
+            r[k] = r[k] - t[i, k] * r[i]
+    lanes = lax.broadcasted_iota(jnp.int32, (s.shape[0] - 8, 128), 1)
+    s = jnp.where((lanes >= at) & (lanes < stop), 0.0, s[8:])
+    for j in range(8):
+        s = s - columns[j][8:] * r[j][0:1, :]
+    return s
 
 
 def invert_factor(m_ref, block_ref, between, after):
     rank = m_ref.shape[0]
+    late = []
+
+    def update(rows, columns, lower, start):
+        if rows.start < rows.stop and columns.start < columns.stop:
+            m_ref[rows, columns] = m_ref[rows, columns] - dot(
+                lower, m_ref[start : start + 128, columns], NN, HIGHEST
+            )
+
     for start in range(0, rank, 128):
         stop = start + 128
         here = slice(start, stop)
-        carry = m_ref[here, here]
-        for quarter in range(4):
-            carry = lax.fori_loop(
-                2 * quarter,
-                2 * quarter + 2,
-                functools.partial(eliminate, w_ref=block_ref),
-                carry,
-            )
-            between()
-        w = [
-            pltpu.roll(block_ref[16 * i : 16 * i + 16, :], 16 * i, 1) if i else block_ref[0:16, :]
-            for i in range(8)
-        ]
-        w = jnp.concatenate(w, axis=0)
+        s = m_ref[here, here]
+        for m in range(16):
+            s = eliminate(m, s, block_ref)
+            if late:
+                late.pop()()
+            if m % 2 == 1:
+                between()
+        w = block_ref[...]
         if rank > 128:
             m_ref[here, :] = dot(w, m_ref[here, :], NN, HIGHEST)
         m_ref[here, here] = w
         if stop < rank:
-            below = slice(stop, rank)
-            lower = m_ref[here, below].T
-            m_ref[below, here] = jnp.zeros((rank - stop, 128), jnp.float32)
-            m_ref[below, :] = m_ref[below, :] - dot(lower, m_ref[here, :], NN, HIGHEST)
+            lower = m_ref[here, stop:rank].T
+            m_ref[stop:rank, here] = jnp.zeros((rank - stop, 128), jnp.float32)
+            near, far = slice(stop, stop + 128), slice(stop + 128, rank)
+            update(near, near, lower[0:128], start)
+            late = [
+                functools.partial(update, *where, start)
+                for where in (
+                    (far, far, lower[128:]),
+                    (far, slice(0, stop + 128), lower[128:]),
+                    (near, far, lower[0:128]),
+                    (near, slice(0, stop), lower[0:128]),
+                )
+            ]
         after(start, m_ref[here, 0:stop])
 
 
@@ -245,12 +247,14 @@
     gain,
     b_ref,
     f_ref,
-    momentum_ref,
-    update_ref,
+    qlow_ref,
+    qsplit_ref,
+    rsplit,
     factor_ref,
     bsplit,
     tsplit,
     fall,
+    fsplit,
     part,
     first_parts,
     last_parts,
@@ -270,7 +274,6 @@
     rpair,
     moving,
     rall,
-    rsplit,
     squares,
     f_send,
     f_recv,
@@ -300,18 +303,28 @@
     enter(here, True)
     gather = Gather(here, fall, f_send, f_recv, f_pair)
     gather.begin()
-    tsplit[0], tsplit[1] = split(b_ref[...].T)
-    bsplit[0], bsplit[1] = split(b_ref[...])
-
-    def product(g):
+
+    def transpose(low, high):
+        columns = slice(128 * low, min(128 * high, b_ref.shape[1]))
+        tsplit[0, columns, :], tsplit[1, columns, :] = split(b_ref[:, columns].T)
+
+    def straight(low, high):
+        columns = slice(128 * low, min(128 * high, b_ref.shape[1]))
+        bsplit[0, :, columns], bsplit[1, :, columns] = split(b_ref[:, columns])
+
+    def join(g):
         for n in range(4 * g, 4 * g + 4):
             gather.shared(n)
         rows = [
             fall[pl.ds(pl.multiple_of(32 * here.chip(offset_of(n)), 32), 32), :]
             for n in range(4 * g, 4 * g + 4)
         ]
-        f = split(jnp.concatenate(rows, axis=0))
-        part[128 * g : 128 * g + 128, :] = dot3(f, (tsplit[0], tsplit[1]), NN)
+        fsplit[0], fsplit[1] = split(jnp.concatenate(rows, axis=0))
+
+    def product(g, turn):
+        rows = slice(128 * g, 128 * g + 128)
+        one = dot(fsplit[turn // 2], tsplit[turn % 2], NN, None)
+        part[rows, :] = part[rows, :] + one if turn else one
 
     def spread(base, rows, parts, turn):
         piece = rows // peers
@@ -347,16 +360,27 @@
             ).start()
 
     early = 128 * last
+    tile = functools.partial
+    pieces = [tile(transpose, at, at + 4) for at in range(0, b_ref.shape[1] // 128, 4)]
+    pieces += [lambda: None] * (4 - len(pieces))
+    for g in range(groups):
+        pieces += [tile(join, g)] + [tile(product, g, turn) for turn in (0, 1, 2)]
+    pieces.reverse()
     for step in range(1, ring + 1):
-        gather.step(step)
-        if step % 2 == 0:
-            product(step // 2 - 1)
-            if step // 2 == last:
-                spread(0, early, first_parts, 0)
-        elif last and step == ring - 1:
-            total(0, early, first_parts, 0)
+        for sub in (0, 1):
+            gather.step(step, sub)
+            pieces.pop()()
+    if last:
+        spread(0, early, first_parts, 0)
+    while pieces:
+        pieces.pop()()
     spread(early, 128, last_parts, 2)
+    if last:
+        total(0, early, first_parts, 0)
+    middle = b_ref.shape[1] // 256
+    straight(0, middle)
     total(early, 128, last_parts, 2)
+    straight(middle, 2 * middle + 1)
     if last:
         await_bytes(first_parts.at[pl.ds(1, peers - 1)], p_recv.at[1])
     await_bytes(last_parts.at[pl.ds(1, peers - 1)], p_recv.at[3])
@@ -386,28 +410,27 @@
         chip = here.chip(offset_of(n))
         return rows16(rpart, chip, here.c, sub)[...] + rpair[n, 8 * sub : 8 * sub + 8, :]
 
-    def scatter(k):
-        if k % 2 == 0:
+    def scatter(k, sub):
+        if k % 2 == 0 and sub == 0:
             g = k // 2 - 1
             await_bytes(rpair.at[pl.ds(4 * g, 4)], pair_recv.at[g])
-        for sub in (0, 1):
-            for way in (0, 1):
-                if k == ring and sub != way:
-                    continue
-                place = moving.at[way, k, pl.ds(8 * sub, 8)]
-                n = 2 * k - 1 if (way == 0 or k == ring) else 2 * k
-                if k < ring - 1 or (k == ring - 1 and sub == way):
-                    await_bytes(place, rs_recv.at[way, k, sub])
-                    place[...] = place[...] + right_own(n, sub)
-                else:
-                    place[...] = right_own(n, sub)
-                remote(
-                    place,
-                    moving.at[way, k - 1, pl.ds(8 * sub, 8)],
-                    rs_send,
-                    rs_recv.at[way, k - 1, sub],
-                    here.at(1 - 2 * way),
-                ).start()
+        for way in (0, 1):
+            if k == ring and sub != way:
+                continue
+            place = moving.at[way, k, pl.ds(8 * sub, 8)]
+            n = 2 * k - 1 if (way == 0 or k == ring) else 2 * k
+            if k < ring - 1 or (k == ring - 1 and sub == way):
+                await_bytes(place, rs_recv.at[way, k, sub])
+                place[...] = place[...] + right_own(n, sub)
+            else:
+                place[...] = right_own(n, sub)
+            remote(
+                place,
+                moving.at[way, k - 1, pl.ds(8 * sub, 8)],
+                rs_send,
+                rs_recv.at[way, k - 1, sub],
+                here.at(1 - 2 * way),
+            ).start()
 
     collect = Gather(here, rall, ag_send, ag_recv, ag_pair)
 
@@ -428,21 +451,20 @@
         place = pl.ds(pl.multiple_of(32 * here.chip(offset_of(n)), 32), 32)
         rsplit[0, place, :], rsplit[1, place, :] = split(rall[place, :])
 
-    def onward(step):
-        collect.step(step)
-        if step == 1:
-            halve(0)
-        else:
-            halve(2 * step - 3)
-            halve(2 * step - 2)
+    def onward(step, sub):
+        collect.step(step, sub)
+        n = 2 * step - 3 + sub
+        if n >= 0:
+            halve(n)
 
     events = []
     for g in range(last, -1, -1):
         events.append(functools.partial(right_product, g))
-        events.append(functools.partial(scatter, 2 * g + 2))
-        events.append(functools.partial(scatter, 2 * g + 1))
+        for k in (2 * g + 2, 2 * g + 1):
+            events += [functools.partial(scatter, k, sub) for sub in (0, 1)]
     events.append(settle)
-    events += [functools.partial(onward, step) for step in range(1, ring + 1)]
+    for step in range(1, ring + 1):
+        events += [functools.partial(onward, step, sub) for sub in (0, 1)]
     events.reverse()
 
     def advance(count=1):
@@ -460,7 +482,7 @@
     keep = pl.ds(pl.multiple_of(half * here.c, half), half)
     pair = remote(gpart.at[theirs], gpair, g_send.at[0], g_recv.at[0], here.partner())
     pair.start()
-    advance()
+    advance(2)
     psplit[0], psplit[1] = split(pt[...])
     pair.wait()
     chip_sum = gpart[keep, :] + gpair[...]
@@ -487,7 +509,7 @@
         place = gsums.at[here.z]
         remote(place, place, g_send.at[2], g_recv.at[2], here.at(k)).start()
 
-    advance(2)
+    advance(3)
     await_bytes(gsums.at[pl.ds(0, chips - 1)], g_recv.at[2])
     gram[here.t, here.c] = gsums[...].reshape(half, rank)
 
@@ -516,7 +538,6 @@
     advance(len(events))
     halve(chips - 1)
 
-    await_bytes(rpart.at[pl.ds(0, rank // 2)], pair_send)
     sums = jnp.zeros((rank, 128), jnp.float32)
     for at, width in tiles:
         columns = slice(at, at + width)
@@ -531,7 +552,6 @@
                 )
             )
         right = jnp.concatenate(blocks, axis=0)
-        rpart[:, columns] = right
         for lane in range(0, width, 128):
             one = right[:, lane : lane + 128]
             sums = sums + one * one
@@ -555,26 +575,18 @@
             )
         )
     q = jnp.concatenate(blocks, axis=0).T
-    q1 = (q * -0.05).astype(jnp.bfloat16)
-    for at, width in tiles:
-        columns = slice(at, at + width)
-        momentum_ref[:, columns] = b_ref[:, columns] + dot(
-            q1, rsplit[0, :, columns], NN, None
-        )
+    qlow_ref[...] = (q * -0.05).astype(jnp.bfloat16)
     await_bytes(squares.at[pl.ds(1, peers - 1)], sq_recv)
     scales = lax.rsqrt(jnp.sum(squares[...], axis=0) * mean + 1e-06)
-    scaled = split(q * (scales * gain))
-    for at, width in tiles:
-        columns = slice(at, at + width)
-        update_ref[:, columns] = dot3(
-            scaled, (rsplit[0, :, columns], rsplit[1, :, columns]), NN
-        ).astype(jnp.bfloat16)
-    lanes = lax.broadcasted_iota(jnp.int32, (16, rank), 1)
-    rows = lax.broadcasted_iota(jnp.int32, (16, rank), 0) + (32 * here.z + 16 * here.c)
-    picked = jnp.where(lanes == rows, jnp.broadcast_to(scales, (16, rank)), 0.0)
-    factor_ref[...] = rows16(rpart, here.z, here.c)[...] * jnp.sum(
-        picked, axis=1, keepdims=True
-    )
+    qsplit_ref[0], qsplit_ref[1] = split(q * (scales * gain))
+    lanes = lax.broadcasted_iota(jnp.int32, (32, rank), 1)
+    rows = lax.broadcasted_iota(jnp.int32, (32, rank), 0) + 32 * here.z
+    picked = jnp.where(lanes == rows, jnp.broadcast_to(scales, (32, rank)), 0.0)
+    place = pl.ds(pl.multiple_of(32 * here.z, 32), 32)
+    ours = (
+        rsplit[0, place, :].astype(jnp.float32) + rsplit[1, place, :].astype(jnp.float32)
+    ) * jnp.sum(picked, axis=1, keepdims=True)
+    factor_ref[...] = jnp.where(here.c == 0, ours[0:16], ours[16:32])
 
     gather.end()
     collect.end()
@@ -586,8 +598,16 @@
     await_bytes(gsplits.at[pl.ds(1, chips - 1)], g_send.at[1])
     await_bytes(gsums.at[pl.ds(0, chips - 1)], g_send.at[2])
     await_bytes(gram.at[pl.ds(0, peers - 1), 0], g_send.at[3])
+    await_bytes(rpart.at[pl.ds(0, rank // 2)], pair_send)
     await_bytes(rall.at[pl.ds(0, 16 * (chips - 1))], rs_send)
     await_bytes(squares.at[pl.ds(1, peers - 1)], sq_send)
+
+
+def finish(b_ref, qlow_ref, qsplit_ref, rsplit_ref, f_ref, momentum_ref, update_ref, factor_ref):
+    right = (rsplit_ref[0], rsplit_ref[1])
+    momentum_ref[...] = b_ref[...] + dot(qlow_ref[...], right[0], NN, None)
+    update_ref[...] = dot3((qsplit_ref[0], qsplit_ref[1]), right, NN).astype(jnp.bfloat16)
+    factor_ref[...] = f_ref[...]
 
 
 def body(chips, peers, buffer, factor):
@@ -601,7 +621,7 @@
     f32, bf16 = jnp.float32, jnp.bfloat16
     dma = pltpu.SemaphoreType.DMA
     vmem = pl.BlockSpec(memory_space=pltpu.VMEM)
-    momentum, update, factor_t = pl.pallas_call(
+    qlow, qsplit, rsplit, factor_t = pl.pallas_call(
         functools.partial(
             kernel,
             chips,
@@ -611,16 +631,18 @@
             math.sqrt(rows * 2 * chips / rank),
         ),
         out_shape=(
-            jax.ShapeDtypeStruct((rows, columns), f32),
-            jax.ShapeDtypeStruct((rows, columns), bf16),
+            jax.ShapeDtypeStruct((rows, rank), bf16),
+            jax.ShapeDtypeStruct((2, rows, rank), bf16),
+            jax.ShapeDtypeStruct((2, rank, columns), bf16),
             jax.ShapeDtypeStruct((16, columns), f32),
         ),
         in_specs=[vmem] * 2,
-        out_specs=(vmem,) * 3,
+        out_specs=(vmem,) * 4,
         scratch_shapes=[
             pltpu.VMEM((2, rows, columns), bf16),
             pltpu.VMEM((2, columns, rows), bf16),
             pltpu.VMEM((rank, columns), f32),
+            pltpu.VMEM((2, 128, columns), bf16),
             pltpu.VMEM((rank, rows), f32),
             pltpu.VMEM((peers, max(groups - 1, 1) * 128 // peers, rows), f32),
             pltpu.VMEM((peers, 128 // peers, rows), f32),
@@ -640,7 +662,6 @@
             pltpu.VMEM((chips, 16, columns), f32),
             pltpu.VMEM((2, ring + 1, 16, columns), f32),
             pltpu.VMEM((rank, columns), f32),
-            pltpu.VMEM((2, rank, columns), bf16),
             pltpu.VMEM((peers, 1, rank), f32),
             dma,
             dma((2, ring, 2)),
@@ -664,6 +685,32 @@
         ),
         name="low_rank_update",
     )(buffer, factor.T)
+
+    def whole(*shape):
+        return pl.BlockSpec(shape, lambda i: (0,) * len(shape))
+
+    def tile(*lead):
+        return pl.BlockSpec((*lead, 256), lambda i: (0,) * len(lead) + (i,))
+
+    momentum, update, factor_t = pl.pallas_call(
+        finish,
+        grid=(pl.cdiv(columns, 256),),
+        out_shape=(
+            jax.ShapeDtypeStruct((rows, columns), f32),
+            jax.ShapeDtypeStruct((rows, columns), bf16),
+            jax.ShapeDtypeStruct((16, columns), f32),
+        ),
+        in_specs=[
+            tile(rows),
+            whole(rows, rank),
+            whole(2, rows, rank),
+            tile(2, rank),
+            tile(16),
+        ],
+        out_specs=(tile(rows), tile(rows), tile(16)),
+        compiler_params=pltpu.CompilerParams(vmem_limit_bytes=LIMIT),
+        name="finish",
+    )(buffer, qlow, qsplit, rsplit, factor_t)
     return momentum, update, factor_t.T
 
 

time: 155 us -> 161 us (1.039)
  Pallas kernels: 148 us -> 160 us
  local copies, waits for them, and re-layouts: 4.38 us -> 0 us
    pallas_call x0 -> x1, Pallas kernels: none -> 7.67 us  [body(): pl.pallas_call(finish, grid=(pl.cdiv(columns, 256),), out_shape=(jax.Shap...]
    unnamed x7 -> x0, local copies, waits for them, and re-layouts: 4.38 us -> none
    pallas_call x1, Pallas kernels: 148 us -> 152 us  [body(): pl.pallas_call(functools.partial(kernel, chips, peers, 1.0 / math.sqrt(to...]
where the time goes in v2:
time: 161 us; the launch traced here: 160 us
  Pallas kernels  160 us (99%)
    pallas_call x1, Pallas kernels, body(): pl.pallas_call(functools.partial(kernel, chips, peers, 1.0 / math.sqrt(to...  152 us
    pallas_call x1, Pallas kernels, body(): pl.pallas_call(finish, grid=(pl.cdiv(columns, 256),), out_shape=(jax.Shap...  7.67 us

profile of v2, /device:TPU:1, one launch (start us, length us, event | category | flops | bytes accessed | tf_op | source)
XLA Modules:
  0.0 160.3 jit_solution(3570564846325102196)
XLA Ops:
  0.6 152.0 %low_rank_update.1 = (bf16[256,512]{1,0:T(8,128)(2,1)}, bf16[2,256,512]{2,1,0:T(8,128)(2,1)}, bf16[2,512,1664]{2,1,0:T(8,128)(2,1)}, f32[16,1664]{1,0:T(8,128)}) custom-call(f32[256,1664]{1,0:T(8,128)} %b_ref.3, f32[16,1664]{1,0:T(8,128)} %bitcast.2), custom_call_target="tpu_custom_call" | custom-call | tf_op jit(solution)/shard_map/low_rank_update/pallas_call | solution.py:624
  152.6 7.7 %finish.1 = (f32[256,1664]{1,0:T(8,128)}, bf16[256,1664]{1,0:T(8,128)(2,1)}, f32[16,1664]{1,0:T(8,128)}) custom-call(f32[256,1664]{1,0:T(8,128)} %b_ref.3, bf16[256,512]{1,0:T(8,128)(2,1)} %get-tuple-element.10.qlow_ref, bf16[2,256,512]{2,1,0:T(8,128)(2,1)} %get-tuple-element.11.qsplit_ref, bf16[2,512,1664]{2,1,0:T(8,128)(2,1)} %get-tuple-element.12.rsplit_ref, ...), custom_call_target="tpu_custom_call" | custom-call | tf_op jit(solution)/shard_map/finish/pallas_call | solution.py:695

commit v3 on v2

--- a/solution.py
+++ b/solution.py
@@ -97,11 +97,6 @@
         self.send, self.recv, self.pair_recv = send, recv, pair_recv
         self.half = here.chips // 2
 
-    def subs(self, step, way):
-        if step < self.half:
-            return (0, 1)
-        return (way,) if step == self.half else ()
-
     def forward(self, step, way, sub):
         here, sign = self.here, 1 - 2 * way
         ref = rows16(self.buf, here.chip(-sign * (step - 1)), here.c, sub)
@@ -122,16 +117,27 @@
 
     def step(self, step, sub):
         here = self.here
-        for way in (0, 1):
-            if sub in self.subs(step, way):
-                sign = 1 - 2 * way
-                ref = rows16(self.buf, here.chip(-sign * step), here.c, sub)
-                await_bytes(ref, self.recv.at[way, step - 1, sub])
-                if sub in self.subs(step + 1, way):
-                    self.forward(step + 1, way, sub)
+
+        def take(way):
+            sign = 1 - 2 * way
+            ref = rows16(self.buf, here.chip(-sign * step), here.c, sub)
+            await_bytes(ref, self.recv.at[way, step - 1, sub])
+
+            @pl.when(step + 1 < self.half + (sub == way))
+            def _():
+                self.forward(step + 1, way, sub)
+
+        take(sub)
+
+        @pl.when(step < self.half)
+        def _():
+            take(1 - sub)
+
         if sub == 1:
             self.share(step, 2 * step - 1)
-            if step < self.half:
+
+            @pl.when(step < self.half)
+            def _():
                 self.share(-step, 2 * step)
 
     def shared(self, n):
@@ -159,80 +165,88 @@
     return jnp.broadcast_to(value, (8, 128))
 
 
-def eliminate(m, s, w_ref):
-    at, stop = 8 * m, 8 * m + 8
+def eliminate(turn, carry, w_ref):
+    s = carry
     lane = lax.broadcasted_iota(jnp.int32, (8, 128), 1)
     sublane = lax.broadcasted_iota(jnp.int32, (8, 128), 0)
-    columns = [jnp.broadcast_to(s[:, at + j : at + j + 1], s.shape) for j in range(8)]
-    d = {(i, j): splat(columns[j][i : i + 1, :]) for j in range(8) for i in range(j, 8)}
-    block = (lane >= at) & (lane < stop)
-    top = jnp.where(block, jnp.where(lane == sublane + at, 1.0, 0.0), s[0:8])
-    r = [splat(top[i : i + 1, :]) for i in range(8)]
-    root, inverse, t = [], [], {}
-    for k in range(8):
-        root.append(lax.rsqrt(d[k, k]))
-        inverse.append(root[k] * root[k])
-        for i in range(k + 1, 8):
-            t[i, k] = d[i, k] * inverse[k]
-            for j in range(k + 1, i + 1):
-                d[i, j] = d[i, j] - t[i, k] * d[j, k]
-            r[i] = r[i] - t[i, k] * r[k]
-    done = r[0] * root[0]
-    for k in range(1, 8):
-        done = jnp.where(sublane == k, r[k] * root[k], done)
-    w_ref[at:stop, :] = jnp.where(lane < stop, done, 0.0)
-    if m == 15:
-        return None
-    for k in range(7, -1, -1):
-        r[k] = r[k] * inverse[k]
-        for i in range(7, k, -1):
-            r[k] = r[k] - t[i, k] * r[i]
-    lanes = lax.broadcasted_iota(jnp.int32, (s.shape[0] - 8, 128), 1)
-    s = jnp.where((lanes >= at) & (lanes < stop), 0.0, s[8:])
-    for j in range(8):
-        s = s - columns[j][8:] * r[j][0:1, :]
-    return s
-
-
-def invert_factor(m_ref, block_ref, between, after):
+    for half in (0, 8):
+        block = (lane >= half) & (lane < half + 8)
+        columns = [
+            jnp.broadcast_to(s[:, half + j : half + j + 1], s.shape) for j in range(8)
+        ]
+        d = {
+            (i, j): splat(columns[j][i : i + 1, :]) for j in range(8) for i in range(j, 8)
+        }
+        top = jnp.where(block, jnp.where(lane == sublane + half, 1.0, 0.0), s[0:8])
+        r = [splat(top[i : i + 1, :]) for i in range(8)]
+        root, inverse, t = [], [], {}
+        for k in range(8):
+            root.append(lax.rsqrt(d[k, k]))
+            inverse.append(root[k] * root[k])
+            for i in range(k + 1, 8):
+                t[i, k] = d[i, k] * inverse[k]
+                for j in range(k + 1, i + 1):
+                    d[i, j] = d[i, j] - t[i, k] * d[j, k]
+                r[i] = r[i] - t[i, k] * r[k]
+        done = r[0] * root[0]
+        for k in range(1, 8):
+            done = jnp.where(sublane == k, r[k] * root[k], done)
+        keep = (lane >= 128 - 16 * turn) | (lane < half + 8)
+        w_ref[pl.ds(pl.multiple_of(16 * turn + half, 8), 8), :] = jnp.where(
+            keep, done, 0.0
+        )
+        for k in range(7, -1, -1):
+            r[k] = r[k] * inverse[k]
+            for i in range(7, k, -1):
+                r[k] = r[k] - t[i, k] * r[i]
+        lanes = lax.broadcasted_iota(jnp.int32, (s.shape[0] - 8, 128), 1)
+        s = jnp.where((lanes >= half) & (lanes < half + 8), 0.0, s[8:])
+        for j in range(8):
+            s = s - columns[j][8:] * r[j][0:1, :]
+    blank = jnp.zeros((16, 128), jnp.float32)
+    return pltpu.roll(jnp.concatenate([s, blank], axis=0), 112, 1)
+
+
+def invert_factor(m_ref, block_ref, wsplit, between):
     rank = m_ref.shape[0]
-    late = []
-
-    def update(rows, columns, lower, start):
-        if rows.start < rows.stop and columns.start < columns.stop:
-            m_ref[rows, columns] = m_ref[rows, columns] - dot(
-                lower, m_ref[start : start + 128, columns], NN, HIGHEST
-            )
-
-    for start in range(0, rank, 128):
-        stop = start + 128
-        here = slice(start, stop)
-        s = m_ref[here, here]
-        for m in range(16):
-            s = eliminate(m, s, block_ref)
-            if late:
-                late.pop()()
-            if m % 2 == 1:
-                between()
-        w = block_ref[...]
-        if rank > 128:
-            m_ref[here, :] = dot(w, m_ref[here, :], NN, HIGHEST)
+
+    @pl.loop(0, rank // 128)
+    def _(panel):
+        here = pl.ds(pl.multiple_of(128 * panel, 128), 128)
+
+        def half(i, carry):
+            for sub in (0, 1):
+                first = 4 * i + 2 * sub
+                carry = lax.fori_loop(
+                    first,
+                    first + 2,
+                    functools.partial(eliminate, w_ref=block_ref),
+                    carry,
+                )
+                between(2 * panel + i + 1, sub)
+            return carry
+
+        lax.fori_loop(0, 2, half, m_ref[here, here])
+        w = jnp.concatenate(
+            [block_ref[0:16, :]]
+            + [pltpu.roll(block_ref[16 * i : 16 * i + 16, :], 16 * i, 1) for i in range(1, 8)],
+            axis=0,
+        )
+        m_ref[here, :] = dot(w, m_ref[here, :], NN, HIGHEST)
         m_ref[here, here] = w
-        if stop < rank:
-            lower = m_ref[here, stop:rank].T
-            m_ref[stop:rank, here] = jnp.zeros((rank - stop, 128), jnp.float32)
-            near, far = slice(stop, stop + 128), slice(stop + 128, rank)
-            update(near, near, lower[0:128], start)
-            late = [
-                functools.partial(update, *where, start)
-                for where in (
-                    (far, far, lower[128:]),
-                    (far, slice(0, stop + 128), lower[128:]),
-                    (near, far, lower[0:128]),
-                    (near, slice(0, stop), lower[0:128]),
-                )
-            ]
-        after(start, m_ref[here, 0:stop])
+
+        @pl.when(panel < rank // 128 - 1)
+        def _():
+            rows = lax.broadcasted_iota(jnp.int32, (rank, 128), 0)
+            below = rows >= 128 * panel + 128
+            lower = jnp.where(below, m_ref[here, :].T, 0.0)
+            m_ref[:, here] = jnp.where(below, 0.0, m_ref[:, here])
+            m_ref[...] = m_ref[...] - dot(lower, m_ref[here, :], NN, HIGHEST)
+
+        lanes = lax.broadcasted_iota(jnp.int32, (128, rank), 1)
+        wsplit[0, here, :], wsplit[1, here, :] = split(
+            jnp.where(lanes < 128 * panel + 128, m_ref[here, :], 0.0)
+        )
 
 
 def column_tiles(columns):
@@ -274,6 +288,7 @@
     rpair,
     moving,
     rall,
+    sums,
     squares,
     f_send,
     f_recv,
@@ -304,25 +319,35 @@
     gather = Gather(here, fall, f_send, f_recv, f_pair)
     gather.begin()
 
-    def transpose(low, high):
-        columns = slice(128 * low, min(128 * high, b_ref.shape[1]))
-        tsplit[0, columns, :], tsplit[1, columns, :] = split(b_ref[:, columns].T)
+    def tile(i):
+        return pl.ds(pl.multiple_of(128 * i, 128), 128)
+
+    count = b_ref.shape[1] // 128
+
+    def transpose(quarter):
+        low, high = quarter * count // 4, (quarter + 1) * count // 4
+
+        @pl.loop(low, high)
+        def _(i):
+            tsplit[0, tile(i), :], tsplit[1, tile(i), :] = split(b_ref[:, tile(i)].T)
 
     def straight(low, high):
-        columns = slice(128 * low, min(128 * high, b_ref.shape[1]))
-        bsplit[0, :, columns], bsplit[1, :, columns] = split(b_ref[:, columns])
+        @pl.loop(low, high)
+        def _(i):
+            bsplit[0, :, tile(i)], bsplit[1, :, tile(i)] = split(b_ref[:, tile(i)])
 
     def join(g):
-        for n in range(4 * g, 4 * g + 4):
+        order = [4 * g + n for n in range(4)]
+        for n in order:
             gather.shared(n)
         rows = [
             fall[pl.ds(pl.multiple_of(32 * here.chip(offset_of(n)), 32), 32), :]
-            for n in range(4 * g, 4 * g + 4)
+            for n in order
         ]
         fsplit[0], fsplit[1] = split(jnp.concatenate(rows, axis=0))
 
     def product(g, turn):
-        rows = slice(128 * g, 128 * g + 128)
+        rows = tile(g)
         one = dot(fsplit[turn // 2], tsplit[turn % 2], NN, None)
         part[rows, :] = part[rows, :] + one if turn else one
 
@@ -360,37 +385,48 @@
             ).start()
 
     early = 128 * last
-    tile = functools.partial
-    pieces = [tile(transpose, at, at + 4) for at in range(0, b_ref.shape[1] // 128, 4)]
-    pieces += [lambda: None] * (4 - len(pieces))
-    for g in range(groups):
-        pieces += [tile(join, g)] + [tile(product, g, turn) for turn in (0, 1, 2)]
-    pieces.reverse()
-    for step in range(1, ring + 1):
-        for sub in (0, 1):
-            gather.step(step, sub)
-            pieces.pop()()
+
+    def piece(g, i):
+        if i == 0:
+            join(g)
+        else:
+            product(g, i - 1)
+
+    @pl.loop(0, groups)
+    def _(g):
+        for i in range(4):
+            gather.step(2 * g + 1 + i // 2, i % 2)
+
+            @pl.when(g == 0)
+            def _():
+                transpose(i)
+
+            @pl.when(g > 0)
+            def _():
+                piece(g - 1, i)
+
     if last:
         spread(0, early, first_parts, 0)
-    while pieces:
-        pieces.pop()()
+    for i in range(4):
+        piece(last, i)
     spread(early, 128, last_parts, 2)
     if last:
         total(0, early, first_parts, 0)
-    middle = b_ref.shape[1] // 256
-    straight(0, middle)
+    straight(0, count // 2)
     total(early, 128, last_parts, 2)
-    straight(middle, 2 * middle + 1)
+    straight(count // 2, count)
     if last:
         await_bytes(first_parts.at[pl.ds(1, peers - 1)], p_recv.at[1])
     await_bytes(last_parts.at[pl.ds(1, peers - 1)], p_recv.at[3])
-    for n in range(chips):
+
+    @pl.loop(0, chips)
+    def _(n):
         place = pl.ds(pl.multiple_of(32 * here.chip(offset_of(n)), 32), 32)
-        pt[place, :] = arrived[32 * n : 32 * n + 32, :]
+        pt[place, :] = arrived[pl.ds(pl.multiple_of(32 * n, 32), 32), :]
 
     def right_product(g):
-        chipped = [here.chip(offset_of(n)) for n in range(4 * g, 4 * g + 4)]
-        p = split(arrived[128 * g : 128 * g + 128, :])
+        chipped = [here.chip(offset_of(4 * g + n)) for n in range(4)]
+        p = split(arrived[tile(g), :])
         for at, width in tiles:
             b = (bsplit[0, :, at : at + width], bsplit[1, :, at : at + width])
             r = dot3(p, b, NN)
@@ -411,19 +447,19 @@
         return rows16(rpart, chip, here.c, sub)[...] + rpair[n, 8 * sub : 8 * sub + 8, :]
 
     def scatter(k, sub):
-        if k % 2 == 0 and sub == 0:
-            g = k // 2 - 1
-            await_bytes(rpair.at[pl.ds(4 * g, 4)], pair_recv.at[g])
-        for way in (0, 1):
-            if k == ring and sub != way:
-                continue
+        def pass_on(way, come):
             place = moving.at[way, k, pl.ds(8 * sub, 8)]
-            n = 2 * k - 1 if (way == 0 or k == ring) else 2 * k
-            if k < ring - 1 or (k == ring - 1 and sub == way):
+            n = 2 * k - 1 if way == 0 else 2 * k - 2 * k // chips
+
+            @pl.when(come)
+            def _():
                 await_bytes(place, rs_recv.at[way, k, sub])
                 place[...] = place[...] + right_own(n, sub)
-            else:
+
+            @pl.when(jnp.logical_not(come))
+            def _():
                 place[...] = right_own(n, sub)
+
             remote(
                 place,
                 moving.at[way, k - 1, pl.ds(8 * sub, 8)],
@@ -431,6 +467,12 @@
                 rs_recv.at[way, k - 1, sub],
                 here.at(1 - 2 * way),
             ).start()
+
+        pass_on(sub, k < ring)
+
+        @pl.when(k < ring)
+        def _():
+            pass_on(1 - sub, k < ring - 1)
 
     collect = Gather(here, rall, ag_send, ag_recv, ag_pair)
 
@@ -453,94 +495,101 @@
 
     def onward(step, sub):
         collect.step(step, sub)
-        n = 2 * step - 3 + sub
-        if n >= 0:
-            halve(n)
-
-    events = []
-    for g in range(last, -1, -1):
-        events.append(functools.partial(right_product, g))
-        for k in (2 * g + 2, 2 * g + 1):
-            events += [functools.partial(scatter, k, sub) for sub in (0, 1)]
-    events.append(settle)
-    for step in range(1, ring + 1):
-        events += [functools.partial(onward, step, sub) for sub in (0, 1)]
-    events.reverse()
-
-    def advance(count=1):
-        for _ in range(count):
-            if events:
-                events.pop()()
-
-    advance()
+
+        @pl.when(2 * step - 3 + sub >= 0)
+        def _():
+            halve(2 * step - 3 + sub)
+
     block = rank // peers
     half = block // 2
     each = half // chips
     mine = pl.ds(pl.multiple_of(block * here.t, block), block)
-    gpart[...] = dot(pt[mine, :], pt[...].T, NN, HIGHEST)
     theirs = pl.ds(pl.multiple_of(half * (1 - here.c), half), half)
     keep = pl.ds(pl.multiple_of(half * here.c, half), half)
-    pair = remote(gpart.at[theirs], gpair, g_send.at[0], g_recv.at[0], here.partner())
-    pair.start()
-    advance(2)
+
+    def gram_pair():
+        return remote(
+            gpart.at[theirs], gpair, g_send.at[0], g_recv.at[0], here.partner()
+        )
+
+    def gram_own():
+        gpart[...] = dot(pt[mine, :], pt[...].T, NN, HIGHEST)
+        gram_pair().start()
+
+    def gram_scatter():
+        gram_pair().wait()
+        chip_sum = gpart[keep, :] + gpair[...]
+        for k in range(chips):
+            gsplit[k] = chip_sum[each * k : each * (k + 1), :]
+
+        @pl.loop(1, chips)
+        def _(k):
+            remote(
+                gsplit.at[here.chip(k)],
+                gsplits.at[k],
+                g_send.at[1],
+                g_recv.at[1],
+                here.at(k),
+            ).start()
+
+        gsplits[0] = gsplit[here.z]
+
+    def gram_gather():
+        await_bytes(gsplits.at[pl.ds(1, chips - 1)], g_recv.at[1])
+        gsums[here.z] = jnp.sum(gsplits[...], axis=0)
+
+        @pl.loop(1, chips)
+        def _(k):
+            place = gsums.at[here.z]
+            remote(place, place, g_send.at[2], g_recv.at[2], here.at(k)).start()
+
+    def gram_spread():
+        await_bytes(gsums.at[pl.ds(0, chips - 1)], g_recv.at[2])
+        gram[here.t, here.c] = gsums[...].reshape(half, rank)
+
+        @pl.loop(1, peers)
+        def _(k):
+            place = gram.at[here.t, here.c]
+            remote(
+                place, place, g_send.at[3], g_recv.at[3], {"tensor": here.peer(k)}
+            ).start()
+
+    gram_steps = (gram_own, gram_scatter, gram_gather, gram_spread)
+
+    @pl.loop(0, groups)
+    def _(turn):
+        g = last - turn
+        right_product(g)
+        for i, step in enumerate(gram_steps):
+            if i < groups:
+
+                @pl.when(turn == i)
+                def _():
+                    step()
+
+        await_bytes(rpair.at[pl.ds(4 * g, 4)], pair_recv.at[g])
+        for k in (2 * g + 2, 2 * g + 1):
+            for sub in (0, 1):
+                scatter(k, sub)
+
+    for i, step in enumerate(gram_steps):
+        if i >= groups:
+            step()
     psplit[0], psplit[1] = split(pt[...])
-    pair.wait()
-    chip_sum = gpart[keep, :] + gpair[...]
-    for k in range(chips):
-        gsplit[k] = chip_sum[each * k : each * (k + 1), :]
-
-    @pl.loop(1, chips)
-    def _(k):
-        remote(
-            gsplit.at[here.chip(k)],
-            gsplits.at[k],
-            g_send.at[1],
-            g_recv.at[1],
-            here.at(k),
-        ).start()
-
-    advance(2)
-    gsplits[0] = gsplit[here.z]
-    await_bytes(gsplits.at[pl.ds(1, chips - 1)], g_recv.at[1])
-    gsums[here.z] = jnp.sum(gsplits[...], axis=0)
-
-    @pl.loop(1, chips)
-    def _(k):
-        place = gsums.at[here.z]
-        remote(place, place, g_send.at[2], g_recv.at[2], here.at(k)).start()
-
-    advance(3)
-    await_bytes(gsums.at[pl.ds(0, chips - 1)], g_recv.at[2])
-    gram[here.t, here.c] = gsums[...].reshape(half, rank)
-
-    @pl.loop(1, peers)
-    def _(k):
-        place = gram.at[here.t, here.c]
-        remote(
-            place, place, g_send.at[3], g_recv.at[3], {"tensor": here.peer(k)}
-        ).start()
-
-    advance(2)
     await_bytes(gram.at[pl.ds(0, peers - 1), 0], g_recv.at[3])
     halves = gram.at[:, here.c]
     pair = remote(halves, halves, g_send.at[4], g_recv.at[4], here.partner())
     pair.start()
-    advance()
+    settle()
     pair.wait()
     m_ref[...] = gram[...].reshape(rank, rank)
-    wsplit[...] = jnp.zeros_like(wsplit)
-
-    def after(start, w):
-        rows, columns = slice(start, start + 128), slice(0, start + 128)
-        wsplit[0, rows, columns], wsplit[1, rows, columns] = split(w)
-
-    invert_factor(m_ref, block_ref, advance, after)
-    advance(len(events))
+    invert_factor(m_ref, block_ref, wsplit, onward)
     halve(chips - 1)
 
-    sums = jnp.zeros((rank, 128), jnp.float32)
-    for at, width in tiles:
-        columns = slice(at, at + width)
+    sums[...] = jnp.zeros_like(sums)
+
+    def right_tile(at, width):
+        columns = pl.ds(at, width)
         blocks = []
         for row in range(0, rank, 256):
             stop = row + 256
@@ -554,9 +603,18 @@
         right = jnp.concatenate(blocks, axis=0)
         for lane in range(0, width, 128):
             one = right[:, lane : lane + 128]
-            sums = sums + one * one
+            sums[...] = sums[...] + one * one
         rsplit[0, :, columns], rsplit[1, :, columns] = split(right)
-    squares[0] = jnp.sum(sums.T, axis=0, keepdims=True)
+
+    full = 256 * (b_ref.shape[1] // 256)
+
+    @pl.loop(0, full // 256)
+    def _(i):
+        right_tile(pl.multiple_of(256 * i, 256), 256)
+
+    if full < b_ref.shape[1]:
+        right_tile(full, b_ref.shape[1] - full)
+    squares[0] = jnp.sum(sums[...].T, axis=0, keepdims=True)
 
     @pl.loop(1, peers)
     def _(k):
@@ -662,6 +720,7 @@
             pltpu.VMEM((chips, 16, columns), f32),
             pltpu.VMEM((2, ring + 1, 16, columns), f32),
             pltpu.VMEM((rank, columns), f32),
+            pltpu.VMEM((rank, 128), f32),
             pltpu.VMEM((peers, 1, rank), f32),
             dma,
             dma((2, ring, 2)),

time: 161 us -> 151 us (0.938)
  Pallas kernels: 160 us -> 150 us
    pallas_call x1, Pallas kernels: 152 us -> 142 us  [body(): pl.pallas_call(functools.partial(kernel, chips, peers, 1.0 / math.sqrt(to...]
where the time goes in v3:
time: 151 us; the launch traced here: 150 us
  Pallas kernels  150 us (99%)
    pallas_call x1, Pallas kernels, body(): pl.pallas_call(functools.partial(kernel, chips, peers, 1.0 / math.sqrt(to...  142 us
    pallas_call x1, Pallas kernels, body(): pl.pallas_call(finish, grid=(pl.cdiv(columns, 256),), out_shape=(jax.Shap...  7.67 us

profile of v3, /device:TPU:1, one launch (start us, length us, event | category | flops | bytes accessed | tf_op | source)
XLA Modules:
  0.0 150.3 jit_solution(11077134690004575843)
XLA Ops:
  0.6 142.0 %low_rank_update.1 = (bf16[256,512]{1,0:T(8,128)(2,1)}, bf16[2,256,512]{2,1,0:T(8,128)(2,1)}, bf16[2,512,1664]{2,1,0:T(8,128)(2,1)}, f32[16,1664]{1,0:T(8,128)}) custom-call(f32[256,1664]{1,0:T(8,128)} %b_ref.3, f32[16,1664]{1,0:T(8,128)} %bitcast.2), custom_call_target="tpu_custom_call" | custom-call | tf_op jit(solution)/shard_map/low_rank_update/pallas_call | solution.py:682
  142.6 7.7 %finish.1 = (f32[256,1664]{1,0:T(8,128)}, bf16[256,1664]{1,0:T(8,128)(2,1)}, f32[16,1664]{1,0:T(8,128)}) custom-call(f32[256,1664]{1,0:T(8,128)} %b_ref.3, bf16[256,512]{1,0:T(8,128)(2,1)} %get-tuple-element.10.qlow_ref, bf16[2,256,512]{2,1,0:T(8,128)(2,1)} %get-tuple-element.11.qsplit_ref, bf16[2,512,1664]{2,1,0:T(8,128)(2,1)} %get-tuple-element.12.rsplit_ref, ...), custom_call_target="tpu_custom_call" | custom-call | tf_op jit(solution)/shard_map/finish/pallas_call | solution.py:754

commit v4 on v3

--- a/solution.py
+++ b/solution.py
@@ -118,22 +118,23 @@
     def step(self, step, sub):
         here = self.here
 
-        def take(way):
+        def take(way, last):
             sign = 1 - 2 * way
             ref = rows16(self.buf, here.chip(-sign * step), here.c, sub)
             await_bytes(ref, self.recv.at[way, step - 1, sub])
 
-            @pl.when(step + 1 < self.half + (sub == way))
+            @pl.when(step < self.half - last)
             def _():
                 self.forward(step + 1, way, sub)
 
-        take(sub)
+        take(sub, 0)
 
         @pl.when(step < self.half)
         def _():
-            take(1 - sub)
-
-        if sub == 1:
+            take(1 - sub, 1)
+
+        @pl.when(sub == 1)
+        def _():
             self.share(step, 2 * step - 1)
 
             @pl.when(step < self.half)
@@ -214,19 +215,16 @@
     def _(panel):
         here = pl.ds(pl.multiple_of(128 * panel, 128), 128)
 
-        def half(i, carry):
-            for sub in (0, 1):
-                first = 4 * i + 2 * sub
-                carry = lax.fori_loop(
-                    first,
-                    first + 2,
-                    functools.partial(eliminate, w_ref=block_ref),
-                    carry,
-                )
-                between(2 * panel + i + 1, sub)
+        def some(i, carry):
+            carry = eliminate(i, carry, block_ref)
+
+            @pl.when(lax.rem(i, 4) < 3)
+            def _():
+                between(6 * panel + i - i // 4)
+
             return carry
 
-        lax.fori_loop(0, 2, half, m_ref[here, here])
+        lax.fori_loop(0, 8, some, m_ref[here, here])
         w = jnp.concatenate(
             [block_ref[0:16, :]]
             + [pltpu.roll(block_ref[16 * i : 16 * i + 16, :], 16 * i, 1) for i in range(1, 8)],
@@ -262,7 +260,8 @@
     b_ref,
     f_ref,
     qlow_ref,
-    qsplit_ref,
+    qtwice_ref,
+    qrest_ref,
     rsplit,
     factor_ref,
     bsplit,
@@ -442,14 +441,17 @@
                 here.partner(),
             ).start()
 
+    def half_rows(sub):
+        return pl.ds(pl.multiple_of(8 * sub, 8), 8)
+
     def right_own(n, sub):
         chip = here.chip(offset_of(n))
-        return rows16(rpart, chip, here.c, sub)[...] + rpair[n, 8 * sub : 8 * sub + 8, :]
+        return rows16(rpart, chip, here.c, sub)[...] + rpair[n, half_rows(sub), :]
 
     def scatter(k, sub):
         def pass_on(way, come):
-            place = moving.at[way, k, pl.ds(8 * sub, 8)]
-            n = 2 * k - 1 if way == 0 else 2 * k - 2 * k // chips
+            place = moving.at[way, k, half_rows(sub)]
+            n = 2 * k - 1 + way * (1 - 2 * k // chips)
 
             @pl.when(come)
             def _():
@@ -462,7 +464,7 @@
 
             remote(
                 place,
-                moving.at[way, k - 1, pl.ds(8 * sub, 8)],
+                moving.at[way, k - 1, half_rows(sub)],
                 rs_send,
                 rs_recv.at[way, k - 1, sub],
                 here.at(1 - 2 * way),
@@ -554,12 +556,16 @@
                 place, place, g_send.at[3], g_recv.at[3], {"tensor": here.peer(k)}
             ).start()
 
-    gram_steps = (gram_own, gram_scatter, gram_gather, gram_spread)
+    gram_steps = (gram_scatter, gram_gather, gram_spread)
+
+    def paired(g):
+        await_bytes(rpair.at[pl.ds(4 * g, 4)], pair_recv.at[g])
+
+    gram_own()
 
     @pl.loop(0, groups)
     def _(turn):
-        g = last - turn
-        right_product(g)
+        right_product(last - turn)
         for i, step in enumerate(gram_steps):
             if i < groups:
 
@@ -567,23 +573,46 @@
                 def _():
                     step()
 
-        await_bytes(rpair.at[pl.ds(4 * g, 4)], pair_recv.at[g])
-        for k in (2 * g + 2, 2 * g + 1):
-            for sub in (0, 1):
-                scatter(k, sub)
+        @pl.when(lax.rem(turn, 2) == 0)
+        def _():
+            paired(last - turn // 2)
+
+        for sub in (0, 1):
+            scatter(ring - turn, sub)
 
     for i, step in enumerate(gram_steps):
         if i >= groups:
             step()
-    psplit[0], psplit[1] = split(pt[...])
+    for g in range(last - (groups + 1) // 2, -1, -1):
+        paired(g)
     await_bytes(gram.at[pl.ds(0, peers - 1), 0], g_recv.at[3])
     halves = gram.at[:, here.c]
     pair = remote(halves, halves, g_send.at[4], g_recv.at[4], here.partner())
     pair.start()
-    settle()
+    for sub in (0, 1):
+        scatter(groups, sub)
+    psplit[0], psplit[1] = split(pt[...])
     pair.wait()
     m_ref[...] = gram[...].reshape(rank, rank)
-    invert_factor(m_ref, block_ref, wsplit, onward)
+
+    def between(n):
+        sub = lax.rem(n, 2)
+
+        @pl.when(n < 2 * last)
+        def _():
+            scatter(last - n // 2, sub)
+
+        @pl.when(n == 2 * last)
+        def _():
+            settle()
+
+        left = n - 2 * last - 1
+
+        @pl.when((left >= 0) & (left < 2 * ring))
+        def _():
+            onward(left // 2 + 1, 1 - sub)
+
+    invert_factor(m_ref, block_ref, wsplit, between)
     halve(chips - 1)
 
     sums[...] = jnp.zeros_like(sums)
@@ -636,7 +665,9 @@
     qlow_ref[...] = (q * -0.05).astype(jnp.bfloat16)
     await_bytes(squares.at[pl.ds(1, peers - 1)], sq_recv)
     scales = lax.rsqrt(jnp.sum(squares[...], axis=0) * mean + 1e-06)
-    qsplit_ref[0], qsplit_ref[1] = split(q * (scales * gain))
+    high, qrest_ref[...] = split(q * (scales * gain))
+    qtwice_ref[:, 0:rank] = high
+    qtwice_ref[:, rank : 2 * rank] = high
     lanes = lax.broadcasted_iota(jnp.int32, (32, rank), 1)
     rows = lax.broadcasted_iota(jnp.int32, (32, rank), 0) + 32 * here.z
     picked = jnp.where(lanes == rows, jnp.broadcast_to(scales, (32, rank)), 0.0)
@@ -661,10 +692,13 @@
     await_bytes(squares.at[pl.ds(1, peers - 1)], sq_send)
 
 
-def finish(b_ref, qlow_ref, qsplit_ref, rsplit_ref, f_ref, momentum_ref, update_ref, factor_ref):
-    right = (rsplit_ref[0], rsplit_ref[1])
-    momentum_ref[...] = b_ref[...] + dot(qlow_ref[...], right[0], NN, None)
-    update_ref[...] = dot3((qsplit_ref[0], qsplit_ref[1]), right, NN).astype(jnp.bfloat16)
+def finish(
+    b_ref, qlow_ref, qtwice_ref, qrest_ref, r_ref, f_ref, momentum_ref, update_ref, factor_ref
+):
+    high = r_ref[0 : qlow_ref.shape[1], :]
+    momentum_ref[...] = b_ref[...] + dot(qlow_ref[...], high, NN, None)
+    update = dot(qtwice_ref[...], r_ref[...], NN, None) + dot(qrest_ref[...], high, NN, None)
+    update_ref[...] = update.astype(jnp.bfloat16)
     factor_ref[...] = f_ref[...]
 
 
@@ -679,7 +713,7 @@
     f32, bf16 = jnp.float32, jnp.bfloat16
     dma = pltpu.SemaphoreType.DMA
     vmem = pl.BlockSpec(memory_space=pltpu.VMEM)
-    qlow, qsplit, rsplit, factor_t = pl.pallas_call(
+    qlow, qtwice, qrest, rsplit, factor_t = pl.pallas_call(
         functools.partial(
             kernel,
             chips,
@@ -690,12 +724,13 @@
         ),
         out_shape=(
             jax.ShapeDtypeStruct((rows, rank), bf16),
-            jax.ShapeDtypeStruct((2, rows, rank), bf16),
+            jax.ShapeDtypeStruct((rows, 2 * rank), bf16),
+            jax.ShapeDtypeStruct((rows, rank), bf16),
             jax.ShapeDtypeStruct((2, rank, columns), bf16),
             jax.ShapeDtypeStruct((16, columns), f32),
         ),
         in_specs=[vmem] * 2,
-        out_specs=(vmem,) * 4,
+        out_specs=(vmem,) * 5,
         scratch_shapes=[
             pltpu.VMEM((2, rows, columns), bf16),
             pltpu.VMEM((2, columns, rows), bf16),
@@ -762,14 +797,15 @@
         in_specs=[
             tile(rows),
             whole(rows, rank),
-            whole(2, rows, rank),
-            tile(2, rank),
+            whole(rows, 2 * rank),
+            whole(rows, rank),
+            tile(2 * rank),
             tile(16),
         ],
         out_specs=(tile(rows), tile(rows), tile(16)),
         compiler_params=pltpu.CompilerParams(vmem_limit_bytes=LIMIT),
         name="finish",
-    )(buffer, qlow, qsplit, rsplit, factor_t)
+    )(buffer, qlow, qtwice, qrest, rsplit.reshape(2 * rank, columns), factor_t)
     return momentum, update, factor_t.T
 
 

time: 151 us -> 158 us (1.046)
  Pallas kernels: 150 us -> 157 us
    pallas_call x1, Pallas kernels: 142 us -> 149 us  [body(): pl.pallas_call(functools.partial(kernel, chips, peers, 1.0 / math.sqrt(to...]
where the time goes in v4:
time: 158 us
  Pallas kernels  157 us (99%)
    pallas_call x1, Pallas kernels, body(): pl.pallas_call(functools.partial(kernel, chips, peers, 1.0 / math.sqrt(to...  149 us
    pallas_call x1, Pallas kernels, body(): pl.pallas_call(finish, grid=(pl.cdiv(columns, 256),), out_shape=(jax.Shap...  7.74 us

profile of v4, /device:TPU:1, one launch (start us, length us, event | category | flops | bytes accessed | tf_op | source)
XLA Modules:
  0.0 157.8 jit_solution(12276200592684018436)
XLA Ops:
  0.6 149.4 %low_rank_update.1 = (bf16[256,512]{1,0:T(8,128)(2,1)}, bf16[256,1024]{1,0:T(8,128)(2,1)}, bf16[256,512]{1,0:T(8,128)(2,1)}, bf16[2,512,1664]{2,1,0:T(8,128)(2,1)}, f32[16,1664]{1,0:T(8,128)}) custom-call(f32[256,1664]{1,0:T(8,128)} %b_ref.3, f32[16,1664]{1,0:T(8,128)} %bitcast.4), custom_call_target="tpu_custom_call" | custom-call | tf_op jit(solution)/shard_map/low_rank_update/pallas_call | solution.py:716
  150.0 7.7 %finish.1 = (f32[256,1664]{1,0:T(8,128)}, bf16[256,1664]{1,0:T(8,128)(2,1)}, f32[16,1664]{1,0:T(8,128)}) custom-call(f32[256,1664]{1,0:T(8,128)} %b_ref.3, bf16[256,512]{1,0:T(8,128)(2,1)} %get-tuple-element.11.qlow_ref, bf16[256,1024]{1,0:T(8,128)(2,1)} %get-tuple-element.12.qtwice_ref, bf16[256,512]{1,0:T(8,128)(2,1)} %get-tuple-element.13.qrest_ref, ...), custom_call_target="tpu_custom_call" | custom-call | tf_op jit(solution)/shard_map/finish/pallas_call | solution.py:789

commit v5 on v3

--- a/solution.py
+++ b/solution.py
@@ -26,6 +26,9 @@
         self.z, self.c = dp // 2, dp % 2
         self.t = lax.axis_index("tensor")
         self.chips, self.peers = chips, peers
+        self.next = {"dp": 2 * self.chip(1) + self.c}
+        self.back = {"dp": 2 * self.chip(-1) + self.c}
+        self.other = {"dp": 2 * self.z + 1 - self.c}
 
     def chip(self, offset):
         return lax.rem(self.z + offset + self.chips, self.chips)
@@ -34,7 +37,10 @@
         return {"dp": 2 * self.chip(offset) + self.c}
 
     def partner(self):
-        return {"dp": 2 * self.z + 1 - self.c}
+        return self.other
+
+    def neighbour(self, way):
+        return self.back if way else self.next
 
     def peer(self, k):
         return lax.rem(self.t + k, self.peers)
@@ -91,18 +97,24 @@
     return ref.at[pl.ds(pl.multiple_of(start + 8 * sub, 8), 8)]
 
 
+def lane_parts(columns, count):
+    tiles = columns // 128
+    cuts = [128 * (tiles * i // count) for i in range(count + 1)]
+    return [pl.ds(a, b - a) for a, b in zip(cuts, cuts[1:]) if b > a]
+
+
 class Gather:
-    def __init__(self, here, buf, send, recv, pair_recv):
-        self.here, self.buf = here, buf
+    def __init__(self, here, buf, parts, send, recv, pair_recv):
+        self.here, self.buf, self.parts = here, buf, parts
         self.send, self.recv, self.pair_recv = send, recv, pair_recv
         self.half = here.chips // 2
 
-    def forward(self, step, way, sub):
+    def forward(self, step, way, sub, h):
         here, sign = self.here, 1 - 2 * way
-        ref = rows16(self.buf, here.chip(-sign * (step - 1)), here.c, sub)
-        remote(
-            ref, ref, self.send, self.recv.at[way, step - 1, sub], here.at(sign)
-        ).start()
+        rows = rows16(self.buf, here.chip(-sign * (step - 1)), here.c, sub)
+        ref = rows.at[:, self.parts[h]]
+        recv = self.recv.at[way, step - 1, 2 * sub + h]
+        remote(ref, ref, self.send, recv, here.neighbour(way)).start()
 
     def share(self, offset, slot):
         here = self.here
@@ -111,27 +123,31 @@
 
     def begin(self):
         for sub in (0, 1):
-            for way in (0, 1):
-                self.forward(1, way, sub)
+            for h in range(len(self.parts)):
+                for way in (0, 1):
+                    self.forward(1, way, sub, h)
         self.share(0, 0)
 
     def step(self, step, sub):
         here = self.here
 
-        def take(way):
+        def take(way, h):
             sign = 1 - 2 * way
-            ref = rows16(self.buf, here.chip(-sign * step), here.c, sub)
-            await_bytes(ref, self.recv.at[way, step - 1, sub])
+            rows = rows16(self.buf, here.chip(-sign * step), here.c, sub)
+            await_bytes(
+                rows.at[:, self.parts[h]], self.recv.at[way, step - 1, 2 * sub + h]
+            )
 
             @pl.when(step + 1 < self.half + (sub == way))
             def _():
-                self.forward(step + 1, way, sub)
-
-        take(sub)
-
-        @pl.when(step < self.half)
-        def _():
-            take(1 - sub)
+                self.forward(step + 1, way, sub, h)
+
+        for h in range(len(self.parts)):
+            take(sub, h)
+
+            @pl.when(step < self.half)
+            def _():
+                take(1 - sub, h)
 
         if sub == 1:
             self.share(step, 2 * step - 1)
@@ -235,13 +251,16 @@
         m_ref[here, :] = dot(w, m_ref[here, :], NN, HIGHEST)
         m_ref[here, here] = w
 
-        @pl.when(panel < rank // 128 - 1)
-        def _():
-            rows = lax.broadcasted_iota(jnp.int32, (rank, 128), 0)
-            below = rows >= 128 * panel + 128
-            lower = jnp.where(below, m_ref[here, :].T, 0.0)
-            m_ref[:, here] = jnp.where(below, 0.0, m_ref[:, here])
-            m_ref[...] = m_ref[...] - dot(lower, m_ref[here, :], NN, HIGHEST)
+        for last in range(rank // 128 - 1):
+
+            @pl.when(panel == last)
+            def _():
+                start, stop = 128 * last, 128 * last + 128
+                lower = m_ref[start:stop, stop:rank].T
+                m_ref[stop:rank, start:stop] = jnp.zeros((rank - stop, 128), jnp.float32)
+                m_ref[stop:rank, :] = m_ref[stop:rank, :] - dot(
+                    lower, m_ref[start:stop, :], NN, HIGHEST
+                )
 
         lanes = lax.broadcasted_iota(jnp.int32, (128, rank), 1)
         wsplit[0, here, :], wsplit[1, here, :] = split(
@@ -259,12 +278,14 @@
     scale,
     mean,
     gain,
-    b_ref,
+    b_hbm,
     f_ref,
     qlow_ref,
     qsplit_ref,
+    r_hbm,
+    factor_ref,
+    b_ref,
     rsplit,
-    factor_ref,
     bsplit,
     tsplit,
     fall,
@@ -306,6 +327,8 @@
     ag_pair,
     sq_send,
     sq_recv,
+    in_sem,
+    out_sem,
 ):
     here = Place(chips, peers)
     rank = 32 * chips
@@ -313,11 +336,15 @@
     groups = chips // 4
     last = groups - 1
     tiles = column_tiles(b_ref.shape[1])
+    load = pltpu.make_async_copy(b_hbm, b_ref, in_sem)
+    load.start()
     own = rows16(fall, here.z, here.c)
     own[...] = f_ref[...]
     enter(here, True)
-    gather = Gather(here, fall, f_send, f_recv, f_pair)
+    halves = lane_parts(b_ref.shape[1], 2)
+    gather = Gather(here, fall, halves, f_send, f_recv, f_pair)
     gather.begin()
+    load.wait()
 
     def tile(i):
         return pl.ds(pl.multiple_of(128 * i, 128), 128)
@@ -442,50 +469,54 @@
                 here.partner(),
             ).start()
 
-    def right_own(n, sub):
+    def right_own(n, sub, lanes):
         chip = here.chip(offset_of(n))
-        return rows16(rpart, chip, here.c, sub)[...] + rpair[n, 8 * sub : 8 * sub + 8, :]
+        rows = rows16(rpart, chip, here.c, sub)
+        return rows[:, lanes] + rpair[n, 8 * sub : 8 * sub + 8, lanes]
 
     def scatter(k, sub):
-        def pass_on(way, come):
-            place = moving.at[way, k, pl.ds(8 * sub, 8)]
+        def pass_on(way, come, h):
+            lanes = halves[h]
+            place = moving.at[way, k, pl.ds(8 * sub, 8), lanes]
             n = 2 * k - 1 if way == 0 else 2 * k - 2 * k // chips
 
             @pl.when(come)
             def _():
-                await_bytes(place, rs_recv.at[way, k, sub])
-                place[...] = place[...] + right_own(n, sub)
+                await_bytes(place, rs_recv.at[way, k, 2 * sub + h])
+                place[...] = place[...] + right_own(n, sub, lanes)
 
             @pl.when(jnp.logical_not(come))
             def _():
-                place[...] = right_own(n, sub)
+                place[...] = right_own(n, sub, lanes)
 
             remote(
                 place,
-                moving.at[way, k - 1, pl.ds(8 * sub, 8)],
+                moving.at[way, k - 1, pl.ds(8 * sub, 8), lanes],
                 rs_send,
-                rs_recv.at[way, k - 1, sub],
-                here.at(1 - 2 * way),
+                rs_recv.at[way, k - 1, 2 * sub + h],
+                here.neighbour(way),
             ).start()
 
-        pass_on(sub, k < ring)
-
-        @pl.when(k < ring)
-        def _():
-            pass_on(1 - sub, k < ring - 1)
-
-    collect = Gather(here, rall, ag_send, ag_recv, ag_pair)
+        for h in range(len(halves)):
+            pass_on(sub, k < ring, h)
+
+            @pl.when(k < ring)
+            def _():
+                pass_on(1 - sub, k < ring - 1, h)
+
+    collect = Gather(here, rall, lane_parts(b_ref.shape[1], 1), ag_send, ag_recv, ag_pair)
 
     def settle():
         for sub in (0, 1):
-            for way in (0, 1):
-                place = moving.at[way, 0, pl.ds(8 * sub, 8)]
-                await_bytes(place, rs_recv.at[way, 0, sub])
-            rows16(rall, here.z, here.c, sub)[...] = (
-                right_own(0, sub)
-                + moving[0, 0, 8 * sub : 8 * sub + 8, :]
-                + moving[1, 0, 8 * sub : 8 * sub + 8, :]
-            )
+            for h, lanes in enumerate(halves):
+                for way in (0, 1):
+                    place = moving.at[way, 0, pl.ds(8 * sub, 8), lanes]
+                    await_bytes(place, rs_recv.at[way, 0, 2 * sub + h])
+                rows16(rall, here.z, here.c, sub)[:, lanes] = (
+                    right_own(0, sub, lanes)
+                    + moving[0, 0, 8 * sub : 8 * sub + 8, lanes]
+                    + moving[1, 0, 8 * sub : 8 * sub + 8, lanes]
+                )
         collect.begin()
 
     def halve(n):
@@ -496,9 +527,9 @@
     def onward(step, sub):
         collect.step(step, sub)
 
-        @pl.when(2 * step - 3 + sub >= 0)
+        @pl.when(2 * step - 5 + sub >= 0)
         def _():
-            halve(2 * step - 3 + sub)
+            halve(2 * step - 5 + sub)
 
     block = rank // peers
     half = block // 2
@@ -577,14 +608,17 @@
             step()
     psplit[0], psplit[1] = split(pt[...])
     await_bytes(gram.at[pl.ds(0, peers - 1), 0], g_recv.at[3])
-    halves = gram.at[:, here.c]
-    pair = remote(halves, halves, g_send.at[4], g_recv.at[4], here.partner())
+    ours = gram.at[:, here.c]
+    pair = remote(ours, ours, g_send.at[4], g_recv.at[4], here.partner())
     pair.start()
     settle()
     pair.wait()
     m_ref[...] = gram[...].reshape(rank, rank)
     invert_factor(m_ref, block_ref, wsplit, onward)
-    halve(chips - 1)
+
+    @pl.loop(chips - 3, chips)
+    def _(n):
+        halve(n)
 
     sums[...] = jnp.zeros_like(sums)
 
@@ -605,6 +639,9 @@
             one = right[:, lane : lane + 128]
             sums[...] = sums[...] + one * one
         rsplit[0, :, columns], rsplit[1, :, columns] = split(right)
+        pltpu.make_async_copy(
+            rsplit.at[:, :, columns], r_hbm.at[:, :, columns], out_sem
+        ).start()
 
     full = 256 * (b_ref.shape[1] // 256)
 
@@ -646,6 +683,7 @@
     ) * jnp.sum(picked, axis=1, keepdims=True)
     factor_ref[...] = jnp.where(here.c == 0, ours[0:16], ours[16:32])
 
+    await_bytes(rsplit, out_sem)
     gather.end()
     collect.end()
     if last:
@@ -679,6 +717,7 @@
     f32, bf16 = jnp.float32, jnp.bfloat16
     dma = pltpu.SemaphoreType.DMA
     vmem = pl.BlockSpec(memory_space=pltpu.VMEM)
+    anywhere = pl.BlockSpec(memory_space=pl.ANY)
     qlow, qsplit, rsplit, factor_t = pl.pallas_call(
         functools.partial(
             kernel,
@@ -694,9 +733,11 @@
             jax.ShapeDtypeStruct((2, rank, columns), bf16),
             jax.ShapeDtypeStruct((16, columns), f32),
         ),
-        in_specs=[vmem] * 2,
-        out_specs=(vmem,) * 4,
+        in_specs=[anywhere, vmem],
+        out_specs=(vmem, vmem, anywhere, vmem),
         scratch_shapes=[
+            pltpu.VMEM((rows, columns), f32),
+            pltpu.VMEM((2, rank, columns), bf16),
             pltpu.VMEM((2, rows, columns), bf16),
             pltpu.VMEM((2, columns, rows), bf16),
             pltpu.VMEM((rank, columns), f32),
@@ -723,7 +764,7 @@
             pltpu.VMEM((rank, 128), f32),
             pltpu.VMEM((peers, 1, rank), f32),
             dma,
-            dma((2, ring, 2)),
+            dma((2, ring, 4)),
             dma((chips,)),
             dma((4,)),
             dma((4,)),
@@ -732,10 +773,12 @@
             dma,
             dma((groups,)),
             dma,
-            dma((2, ring, 2)),
+            dma((2, ring, 4)),
             dma,
-            dma((2, ring, 2)),
+            dma((2, ring, 4)),
             dma((chips,)),
+            dma,
+            dma,
             dma,
             dma,
         ],

time: 151 us -> 146 us (0.967)
  Pallas kernels: 150 us -> 145 us
    pallas_call x1, Pallas kernels: 142 us -> 138 us  [body(): pl.pallas_call(functools.partial(kernel, chips, peers, 1.0 / math.sqrt(to...]
where the time goes in v5:
time: 146 us
  Pallas kernels  145 us (99%)
    pallas_call x1, Pallas kernels, body(): pl.pallas_call(functools.partial(kernel, chips, peers, 1.0 / math.sqrt(to...  138 us
    pallas_call x1, Pallas kernels, body(): pl.pallas_call(finish, grid=(pl.cdiv(columns, 256),), out_shape=(jax.Shap...  7.67 us

profile of v5, /device:TPU:1, one launch (start us, length us, event | category | flops | bytes accessed | tf_op | source)
XLA Modules:
  0.0 146.0 jit_solution(6181045521603263159)
XLA Ops:
  0.6 137.7 %low_rank_update.1 = (bf16[256,512]{1,0:T(8,128)(2,1)}, bf16[2,256,512]{2,1,0:T(8,128)(2,1)}, bf16[2,512,1664]{2,1,0:T(8,128)(2,1)}, f32[16,1664]{1,0:T(8,128)}) custom-call(f32[256,1664]{1,0:T(8,128)} %b_ref.1, f32[16,1664]{1,0:T(8,128)} %bitcast.2), custom_call_target="tpu_custom_call" | custom-call | tf_op jit(solution)/shard_map/low_rank_update/pallas_call | solution.py:721
  138.3 7.7 %finish.1 = (f32[256,1664]{1,0:T(8,128)}, bf16[256,1664]{1,0:T(8,128)(2,1)}, f32[16,1664]{1,0:T(8,128)}) custom-call(f32[256,1664]{1,0:T(8,128)} %b_ref.1, bf16[256,512]{1,0:T(8,128)(2,1)} %get-tuple-element.10.qlow_ref, bf16[2,256,512]{2,1,0:T(8,128)(2,1)} %get-tuple-element.11.qsplit_ref, bf16[2,512,1664]{2,1,0:T(8,128)(2,1)} %get-tuple-element.12.rsplit_ref, ...), custom_call_target="tpu_custom_call" | custom-call | tf_op jit(solution)/shard_map/finish/pallas_call | solution.py:797

commit v6 on v5

--- a/solution.py
+++ b/solution.py
@@ -230,19 +230,15 @@
     def _(panel):
         here = pl.ds(pl.multiple_of(128 * panel, 128), 128)
 
-        def half(i, carry):
-            for sub in (0, 1):
-                first = 4 * i + 2 * sub
-                carry = lax.fori_loop(
-                    first,
-                    first + 2,
-                    functools.partial(eliminate, w_ref=block_ref),
-                    carry,
-                )
-                between(2 * panel + i + 1, sub)
-            return carry
-
-        lax.fori_loop(0, 2, half, m_ref[here, here])
+        carry = m_ref[here, here]
+        for first in (0, 2, 4, 6):
+            carry = lax.fori_loop(
+                first,
+                first + 2,
+                functools.partial(eliminate, w_ref=block_ref),
+                carry[: 128 - 16 * first],
+            )
+            between(2 * panel + first // 4 + 1, first // 2 % 2)
         w = jnp.concatenate(
             [block_ref[0:16, :]]
             + [pltpu.roll(block_ref[16 * i : 16 * i + 16, :], 16 * i, 1) for i in range(1, 8)],
@@ -585,12 +581,29 @@
                 place, place, g_send.at[3], g_recv.at[3], {"tensor": here.peer(k)}
             ).start()
 
-    gram_steps = (gram_own, gram_scatter, gram_gather, gram_spread)
+    def gram_pass():
+        ours = gram.at[:, here.c]
+        return remote(ours, ours, g_send.at[4], g_recv.at[4], here.partner())
+
+    def gram_share():
+        await_bytes(gram.at[pl.ds(0, peers - 1), 0], g_recv.at[3])
+        gram_pass().start()
+
+    gram_steps = (gram_scatter, gram_gather, gram_spread, gram_share)
+    right_product(last)
+    gram_own()
 
     @pl.loop(0, groups)
     def _(turn):
         g = last - turn
-        right_product(g)
+        await_bytes(rpair.at[pl.ds(4 * g, 4)], pair_recv.at[g])
+        for sub in (0, 1):
+            scatter(2 * g + 2, sub)
+
+        @pl.when(g > 0)
+        def _():
+            right_product(g - 1)
+
         for i, step in enumerate(gram_steps):
             if i < groups:
 
@@ -598,21 +611,15 @@
                 def _():
                     step()
 
-        await_bytes(rpair.at[pl.ds(4 * g, 4)], pair_recv.at[g])
-        for k in (2 * g + 2, 2 * g + 1):
-            for sub in (0, 1):
-                scatter(k, sub)
+        for sub in (0, 1):
+            scatter(2 * g + 1, sub)
 
     for i, step in enumerate(gram_steps):
         if i >= groups:
             step()
     psplit[0], psplit[1] = split(pt[...])
-    await_bytes(gram.at[pl.ds(0, peers - 1), 0], g_recv.at[3])
-    ours = gram.at[:, here.c]
-    pair = remote(ours, ours, g_send.at[4], g_recv.at[4], here.partner())
-    pair.start()
     settle()
-    pair.wait()
+    gram_pass().wait()
     m_ref[...] = gram[...].reshape(rank, rank)
     invert_factor(m_ref, block_ref, wsplit, onward)
 

time: 146 us -> 146 us (level)
  no operation moved by 1% of the time
where the time goes in v6:
time: 146 us
  Pallas kernels  145 us (99%)
    pallas_call x1, Pallas kernels, body(): pl.pallas_call(functools.partial(kernel, chips, peers, 1.0 / math.sqrt(to...  137 us
    pallas_call x1, Pallas kernels, body(): pl.pallas_call(finish, grid=(pl.cdiv(columns, 256),), out_shape=(jax.Shap...  7.67 us

profile of v6, /device:TPU:1, one launch (start us, length us, event | category | flops | bytes accessed | tf_op | source)
XLA Modules:
  0.0 145.7 jit_solution(18201105228132157021)
XLA Ops:
  0.6 137.4 %low_rank_update.1 = (bf16[256,512]{1,0:T(8,128)(2,1)}, bf16[2,256,512]{2,1,0:T(8,128)(2,1)}, bf16[2,512,1664]{2,1,0:T(8,128)(2,1)}, f32[16,1664]{1,0:T(8,128)}) custom-call(f32[256,1664]{1,0:T(8,128)} %b_ref.1, f32[16,1664]{1,0:T(8,128)} %bitcast.2), custom_call_target="tpu_custom_call" | custom-call | tf_op jit(solution)/shard_map/low_rank_update/pallas_call | solution.py:728
  138.0 7.7 %finish.1 = (f32[256,1664]{1,0:T(8,128)}, bf16[256,1664]{1,0:T(8,128)(2,1)}, f32[16,1664]{1,0:T(8,128)}) custom-call(f32[256,1664]{1,0:T(8,128)} %b_ref.1, bf16[256,512]{1,0:T(8,128)(2,1)} %get-tuple-element.10.qlow_ref, bf16[2,256,512]{2,1,0:T(8,128)(2,1)} %get-tuple-element.11.qsplit_ref, bf16[2,512,1664]{2,1,0:T(8,128)(2,1)} %get-tuple-element.12.rsplit_ref, ...), custom_call_target="tpu_custom_call" | custom-call | tf_op jit(solution)/shard_map/finish/pallas_call | solution.py:804

commit v7 on v6

--- a/solution.py
+++ b/solution.py
@@ -337,7 +337,7 @@
     own = rows16(fall, here.z, here.c)
     own[...] = f_ref[...]
     enter(here, True)
-    halves = lane_parts(b_ref.shape[1], 2)
+    halves = lane_parts(b_ref.shape[1], 1)
     gather = Gather(here, fall, halves, f_send, f_recv, f_pair)
     gather.begin()
     load.wait()
@@ -799,11 +799,11 @@
         return pl.BlockSpec(shape, lambda i: (0,) * len(shape))
 
     def tile(*lead):
-        return pl.BlockSpec((*lead, 256), lambda i: (0,) * len(lead) + (i,))
+        return pl.BlockSpec((*lead, 512), lambda i: (0,) * len(lead) + (i,))
 
     momentum, update, factor_t = pl.pallas_call(
         finish,
-        grid=(pl.cdiv(columns, 256),),
+        grid=(pl.cdiv(columns, 512),),
         out_shape=(
             jax.ShapeDtypeStruct((rows, columns), f32),
             jax.ShapeDtypeStruct((rows, columns), bf16),

time: 146 us -> 148 us (1.014)
  Pallas kernels: 145 us -> 148 us
    pallas_call x1, Pallas kernels: 137 us -> 141 us  [body(): pl.pallas_call(functools.partial(kernel, chips, peers, 1.0 / math.sqrt(to...]
where the time goes in v7:
time: 148 us
  Pallas kernels  148 us (100%)
    pallas_call x1, Pallas kernels, body(): pl.pallas_call(functools.partial(kernel, chips, peers, 1.0 / math.sqrt(to...  141 us
    pallas_call x1, Pallas kernels, body(): pl.pallas_call(finish, grid=(pl.cdiv(columns, 512),), out_shape=(jax.Shap...  6.21 us

profile of v7, /device:TPU:1, one launch (start us, length us, event | category | flops | bytes accessed | tf_op | source)
XLA Modules:
  0.0 148.2 jit_solution(4752881069037862851)
XLA Ops:
  0.6 141.4 %low_rank_update.1 = (bf16[256,512]{1,0:T(8,128)(2,1)}, bf16[2,256,512]{2,1,0:T(8,128)(2,1)}, bf16[2,512,1664]{2,1,0:T(8,128)(2,1)}, f32[16,1664]{1,0:T(8,128)}) custom-call(f32[256,1664]{1,0:T(8,128)} %b_ref.1, f32[16,1664]{1,0:T(8,128)} %bitcast.2), custom_call_target="tpu_custom_call" | custom-call | tf_op jit(solution)/shard_map/low_rank_update/pallas_call | solution.py:728
  142.0 6.2 %finish.1 = (f32[256,1664]{1,0:T(8,128)}, bf16[256,1664]{1,0:T(8,128)(2,1)}, f32[16,1664]{1,0:T(8,128)}) custom-call(f32[256,1664]{1,0:T(8,128)} %b_ref.1, bf16[256,512]{1,0:T(8,128)(2,1)} %get-tuple-element.10.qlow_ref, bf16[2,256,512]{2,1,0:T(8,128)(2,1)} %get-tuple-element.11.qsplit_ref, bf16[2,512,1664]{2,1,0:T(8,128)(2,1)} %get-tuple-element.12.rsplit_ref, ...), custom_call_target="tpu_custom_call" | custom-call | tf_op jit(solution)/shard_map/finish/pallas_call | solution.py:804

commit v8 on v7

--- a/solution.py
+++ b/solution.py
@@ -337,7 +337,7 @@
     own = rows16(fall, here.z, here.c)
     own[...] = f_ref[...]
     enter(here, True)
-    halves = lane_parts(b_ref.shape[1], 1)
+    halves = lane_parts(b_ref.shape[1], 2)
     gather = Gather(here, fall, halves, f_send, f_recv, f_pair)
     gather.begin()
     load.wait()

time: 148 us -> 144 us (0.973)
  Pallas kernels: 148 us -> 144 us
    pallas_call x1, Pallas kernels: 141 us -> 137 us  [body(): pl.pallas_call(functools.partial(kernel, chips, peers, 1.0 / math.sqrt(to...]
where the time goes in v8:
time: 144 us
  Pallas kernels  144 us (100%)
    pallas_call x1, Pallas kernels, body(): pl.pallas_call(functools.partial(kernel, chips, peers, 1.0 / math.sqrt(to...  137 us
    pallas_call x1, Pallas kernels, body(): pl.pallas_call(finish, grid=(pl.cdiv(columns, 512),), out_shape=(jax.Shap...  6.21 us

profile of v8, /device:TPU:1, one launch (start us, length us, event | category | flops | bytes accessed | tf_op | source)
XLA Modules:
  0.0 144.2 jit_solution(4841464250080169533)
XLA Ops:
  0.6 137.4 %low_rank_update.1 = (bf16[256,512]{1,0:T(8,128)(2,1)}, bf16[2,256,512]{2,1,0:T(8,128)(2,1)}, bf16[2,512,1664]{2,1,0:T(8,128)(2,1)}, f32[16,1664]{1,0:T(8,128)}) custom-call(f32[256,1664]{1,0:T(8,128)} %b_ref.1, f32[16,1664]{1,0:T(8,128)} %bitcast.2), custom_call_target="tpu_custom_call" | custom-call | tf_op jit(solution)/shard_map/low_rank_update/pallas_call | solution.py:728
  138.0 6.2 %finish.1 = (f32[256,1664]{1,0:T(8,128)}, bf16[256,1664]{1,0:T(8,128)(2,1)}, f32[16,1664]{1,0:T(8,128)}) custom-call(f32[256,1664]{1,0:T(8,128)} %b_ref.1, bf16[256,512]{1,0:T(8,128)(2,1)} %get-tuple-element.10.qlow_ref, bf16[2,256,512]{2,1,0:T(8,128)(2,1)} %get-tuple-element.11.qsplit_ref, bf16[2,512,1664]{2,1,0:T(8,128)(2,1)} %get-tuple-element.12.rsplit_ref, ...), custom_call_target="tpu_custom_call" | custom-call | tf_op jit(solution)/shard_map/finish/pallas_call | solution.py:804
